TPU v7x, 128 devices: a whole 4x4x4 slice. The times are simulated.
128 devices in a mesh: depth: 8 (over y, core), seg: 16 (over z, x).
Axes of the slice: x: 4, y: 4, z: 4, core: 2. Of those that a mesh axis runs over, the one named last changes fastest.
Arguments:
- queries: bfloat16 [8, 16, 128, 2560], P('depth', 'seg'), may hold values from -6 to 6, as said below
- keys_values: bfloat16 [8, 16, 2, 128, 512], P('depth', 'seg'), may hold values from -6 to 6
- grad_out: bfloat16 [8, 16, 128, 2560], P('depth', 'seg'), may hold values from -6 to 6
- parents: int32 [7, 16, 1], replicated, may hold values from 0 to 15
Outputs:
- grad_queries: bfloat16 [8, 16, 128, 2560], P('depth', 'seg')
- grad_keys_values: bfloat16 [8, 16, 2, 128, 512], P('depth', 'seg')
Inputs may be any that keep to these rules, and one draw needn't show every extreme that they name: `queries`: a few query rows and key rows may be nearly parallel in some draws. `parents`: every column of a level is somebody's parent in some level.
All inputs are finite; a program needn't handle non-finite values.
Results may differ from a plain program's by a relative error of at most 0.012.
Values may be sent and summed in bfloat16 or wider, within the bound.
A program may use at most 128 MiB of HBM per device.

v0:
```python
import functools

import jax
import jax.numpy as jnp
from jax import lax
from jax.experimental import pallas as pl
from jax.experimental.pallas import tpu as pltpu
from jax.sharding import PartitionSpec as P

HEADS = 20
KV_HEADS = 4
HEAD_DIM = 128
GROUP = HEADS // KV_HEADS
ROWS = 128
LEVELS = 8
SEGS = 16
PIECE = 16
PIECES_PER_PART = ROWS // PIECE
STACK = GROUP * ROWS
PAIR = 2 * ROWS
TILE = SEGS * PIECE

NEG_FILL = -1e30
SCALE = HEAD_DIM ** -0.5
EXP2_SCALE = SCALE * 1.4426950408889634
MESH = pl.DeviceIdType.MESH
BF16 = jnp.bfloat16
F32 = jnp.float32


def half(value):
    return lax.div(value, 2)


def odd(value):
    return lax.rem(value, 2)


def wrapped(index):
    return jnp.where(index >= SEGS, index - SEGS, index)


def lanes(index, count=1):
    width = count * HEAD_DIM
    return pl.ds(pl.multiple_of(index * width, width), width)


def rows_of(index, count):
    return pl.ds(pl.multiple_of(index * count, count), count)


def fold(tile):
    return tile.reshape(tile.shape[0] // 8, 8, tile.shape[1])


def kernel(
    parents, queries, keys_values, grad_out, grad_queries, grad_kv,
    anc, pick, spread, kv_in, q_in, g_in, kv_stage, pieces, chosen, blocks,
    terms, term_pieces, own, stacks, turned, query_sum, stats, logits, grad_probs,
    probs, grad_logits, total_sum, final_out, final_in,
    kv_sem, q_sem, g_sem, ready, p1_send, p1_recv, p3_send, p3_recv, b1_send, b1_recv,
    f_send, f_recv,
):
    level = lax.axis_index("depth")
    me = lax.axis_index("seg")
    below = LEVELS - 1 - level

    def remote(src, dst, send_sem, recv_sem, device):
        return pltpu.make_async_remote_copy(
            src_ref=src, dst_ref=dst, send_sem=send_sem, recv_sem=recv_sem,
            device_id=device, device_id_type=MESH,
        )

    def wait_bytes(ref, sem):
        pltpu.make_async_copy(ref, ref, sem).wait()

    def per_count(which, action):
        for count in range(1, LEVELS):
            pl.when(which == count)(functools.partial(action, count))

    load_kv = pltpu.make_async_copy(keys_values, kv_in, kv_sem)
    load_q = pltpu.make_async_copy(queries, q_in, q_sem)
    load_g = pltpu.make_async_copy(grad_out, g_in, g_sem)
    load_kv.start()
    load_q.start()
    load_g.start()

    barrier = pltpu.get_barrier_semaphore()

    def in_line(step):
        other = level + step
        return (jnp.where(other >= LEVELS, other - LEVELS, other), me)

    @pl.loop(1, SEGS)
    def _(step):
        pl.semaphore_signal(
            barrier, inc=1, device_id=(level, wrapped(me + step)), device_id_type=MESH
        )

    @pl.loop(1, LEVELS)
    def _(step):
        pl.semaphore_signal(barrier, inc=1, device_id=in_line(step), device_id_type=MESH)

    @pl.loop(0, SEGS)
    def _(column):
        anc[0, column] = column

    @pl.loop(1, below + 1)
    def _(offset):
        @pl.loop(0, SEGS)
        def _(column):
            anc[offset, column] = anc[offset - 1, parents[level + offset - 1, 0, column]]

    load_kv.wait()
    for head in range(KV_HEADS):
        for part in range(2):
            kv_stage[head, pl.ds(part * PIECES_PER_PART, PIECES_PER_PART)] = kv_in[
                0, 0, part, :, head * HEAD_DIM:(head + 1) * HEAD_DIM
            ].reshape(PIECES_PER_PART, PIECE, HEAD_DIM)
    pl.semaphore_wait(barrier, SEGS - 1 + LEVELS - 1)

    def spread_out(group, heads):
        @pl.loop(1, SEGS)
        def _(step):
            peer = wrapped(me + step)
            remote(
                kv_stage.at[heads, peer], pieces.at[heads, me],
                p1_send.at[group], p1_recv.at[group], (level, peer),
            ).start()

        pltpu.make_async_copy(
            kv_stage.at[heads, me], pieces.at[heads, me], p1_recv.at[group]
        ).start()

    groups = (pl.ds(0, 1), pl.ds(1, KV_HEADS - 1))
    for group, heads in enumerate(groups):
        spread_out(group, heads)

    @pl.loop(1, LEVELS)
    def _(step):
        pl.semaphore_signal(ready, inc=1, device_id=in_line(step), device_id_type=MESH)

    @pl.loop(1, below + 1)
    def _(offset):
        lane = lax.broadcasted_iota(jnp.int32, (PIECE, TILE), 1)
        row = lax.broadcasted_iota(jnp.int32, (PIECE, TILE), 0)
        ahead = lane - row
        for column in range(SEGS):
            pick[offset, rows_of(column, PIECE), :] = jnp.where(
                ahead == anc[offset, column] * PIECE, 1.0, 0.0
            ).astype(BF16)

    def pick_and_send(head):
        @pl.loop(1, below + 1)
        def _(offset):
            found = jnp.dot(
                pick[offset], pieces[head].reshape(TILE, HEAD_DIM), preferred_element_type=F32
            )
            chosen[head, offset - 1] = found.astype(BF16).reshape(SEGS, PIECE, HEAD_DIM)

        @pl.loop(0, SEGS)
        def _(step):
            column = wrapped(me + step)

            @pl.loop(1, below + 1)
            def _(offset):
                remote(
                    chosen.at[head, offset - 1, column], blocks.at[head, offset, me],
                    p3_send.at[head], p3_recv.at[head], (level + offset, column),
                ).start()

    wait_bytes(pieces.at[groups[0]], p1_recv.at[0])
    pl.semaphore_wait(ready, LEVELS - 1)

    @pl.loop(0, KV_HEADS)
    def _(head):
        @pl.when(head == 1)
        def _():
            wait_bytes(pieces.at[groups[1]], p1_recv.at[1])

        pick_and_send(head)

    @pl.loop(0, KV_HEADS)
    def _(head):
        blocks[head, 0] = kv_stage[head]

        @pl.when(odd(level) == 0)
        def _():
            blocks[head, level + 1] = jnp.zeros((SEGS, PIECE, HEAD_DIM), BF16)

    @pl.loop(1, below + 1)
    def _(offset):
        lane = lax.broadcasted_iota(jnp.int32, (PIECE, TILE), 1)
        row = lax.broadcasted_iota(jnp.int32, (PIECE, TILE), 0)
        lane_column = lane >> 4
        target = (lane & (PIECE - 1)) - row
        for column in range(SEGS):
            target = jnp.where(
                lane_column == column, target + anc[offset, column] * PIECE, target
            )
        for column in range(SEGS):
            spread[offset, rows_of(column, PIECE), :] = jnp.where(
                target == column * PIECE, 1.0, 0.0
            ).astype(BF16)

    load_q.wait()
    load_g.wait()
    halves = [pl.ds(part * PIECES_PER_PART, PIECES_PER_PART) for part in range(2)]

    def attend(head):
        pairs = half(level) + 1
        span_all = [pl.ds(group * ROWS, ROWS) for group in range(GROUP)]

        def block_pair(pair, part):
            return blocks[head, pl.ds(2 * pair, 2), halves[part]].reshape(PAIR, HEAD_DIM)

        stats[0] = jnp.full((8, STACK), NEG_FILL, F32)
        for index in range(2):
            for group, span in enumerate(span_all):
                tile = (q_in, g_in)[index][0, 0, :, lanes(head * GROUP + group)]
                stacks[index, span, :] = tile
                turned[index, :, span] = tile.T

        @pl.loop(0, pairs)
        def _(pair):
            span_rows = rows_of(pair, PAIR)
            logits[span_rows, :] = jnp.dot(
                block_pair(pair, 0), turned[0], preferred_element_type=F32
            )
            grad_probs[span_rows, :] = jnp.dot(
                block_pair(pair, 1), turned[1], preferred_element_type=F32
            )

            @pl.when(pair == 0)
            def _():
                u_row = lax.broadcasted_iota(jnp.int32, (ROWS, ROWS), 0)
                t_row = lax.broadcasted_iota(jnp.int32, (ROWS, ROWS), 1)
                for span in span_all:
                    logits[0:ROWS, span] = jnp.where(
                        u_row <= t_row, logits[0:ROWS, span], NEG_FILL
                    )

            @pl.when((pair == pairs - 1) & (odd(level) == 0))
            def _():
                logits[rows_of(level + 1, ROWS), :] = jnp.full((ROWS, STACK), NEG_FILL, F32)

            for span in span_all:
                stats[0, :, span] = jnp.maximum(
                    stats[0, :, span], fold(logits[span_rows, span]).max(0)
                )

        stats[1] = jnp.zeros((8, STACK), F32)
        stats[2] = jnp.zeros((8, STACK), F32)
        stats[0] = jnp.broadcast_to(stats[0].max(0, keepdims=True), (8, STACK))

        @pl.loop(0, pairs)
        def _(pair):
            span_rows = rows_of(pair, PAIR)
            for span in span_all:
                top = stats[0, 0:1, span]
                tile = jnp.exp2((logits[span_rows, span] - top) * EXP2_SCALE)
                logits[span_rows, span] = tile
                stats[1, :, span] += fold(tile).sum(0)
                stats[2, :, span] += fold(tile * grad_probs[span_rows, span]).sum(0)

        inverse = 1.0 / stats[1].sum(0, keepdims=True)
        delta = stats[2].sum(0, keepdims=True) * inverse
        stats[1] = jnp.broadcast_to(inverse, (8, STACK))
        stats[2] = jnp.broadcast_to(delta, (8, STACK))
        query_sum[...] = jnp.zeros((HEAD_DIM, STACK), F32)

        @pl.loop(0, pairs)
        def _(pair):
            span_rows = rows_of(pair, PAIR)
            for span in span_all:
                exact = logits[span_rows, span] * stats[1, 0:1, span]
                probs[:, span] = exact.astype(BF16)
                grad_logits[:, span] = (
                    exact * (grad_probs[span_rows, span] - stats[2, 0:1, span])
                ).astype(BF16)
            value_term = jnp.dot(probs[...], stacks[1], preferred_element_type=F32)
            key_term = SCALE * jnp.dot(
                grad_logits[...], stacks[0], preferred_element_type=F32
            )
            for part, term in enumerate((key_term, value_term)):
                cut = term.astype(BF16).reshape(2, PIECES_PER_PART, PIECE, HEAD_DIM)
                terms[head, pl.ds(2 * pair, 2), halves[part]] = cut

                @pl.when(pair == 0)
                def _():
                    own[head, part] = term[0:ROWS]

            query_sum[...] += lax.dot_general(
                block_pair(pair, 0), grad_logits[...], (((0,), (0,)), ((), ())),
                preferred_element_type=F32,
            )

        for group, span in enumerate(span_all):
            grad_queries[0, 0, :, lanes(head * GROUP + group)] = (
                SCALE * query_sum[:, span].T
            ).astype(BF16)

    def send_terms(head):
        @pl.loop(0, SEGS)
        def _(step):
            peer = wrapped(me + step)

            @pl.loop(1, level + 1)
            def _(offset):
                remote(
                    terms.at[head, offset, peer], term_pieces.at[head, offset - 1, me],
                    b1_send.at[head], b1_recv.at[head], (level - offset, peer),
                ).start()

    def sum_and_return(head):
        @pl.when(level < LEVELS - 1)
        def _():
            per_count(
                below,
                lambda count: wait_bytes(
                    term_pieces.at[head, pl.ds(0, count)], b1_recv.at[head]
                ),
            )
            total_sum[...] = jnp.zeros((TILE, HEAD_DIM), F32)

            @pl.loop(1, below + 1)
            def _(offset):
                total_sum[...] += jnp.dot(
                    spread[offset], term_pieces[head, offset - 1].reshape(TILE, HEAD_DIM),
                    preferred_element_type=F32,
                )

            final_out[head] = total_sum[...].astype(BF16).reshape(SEGS, PIECE, HEAD_DIM)

            @pl.loop(1, SEGS)
            def _(step):
                peer = wrapped(me + step)
                remote(
                    final_out.at[head, peer], final_in.at[head, me],
                    f_send.at[head], f_recv.at[head], (level, peer),
                ).start()

            pltpu.make_async_copy(
                final_out.at[head, me], final_in.at[head, me], f_recv.at[head]
            ).start()

    def store(head):
        @pl.when(level < LEVELS - 1)
        def _():
            wait_bytes(final_in.at[head], f_recv.at[head])
            for part in range(2):
                own[head, part] += final_in[head, halves[part]].reshape(
                    ROWS, HEAD_DIM
                ).astype(F32)

        grad_kv[0, 0, :, :, lanes(head)] = own[head].astype(BF16)

    @pl.loop(0, KV_HEADS + 2)
    def _(tick):
        @pl.when(tick < KV_HEADS)
        def _():
            per_count(
                level,
                lambda count: wait_bytes(blocks.at[tick, pl.ds(1, count)], p3_recv.at[tick]),
            )
            attend(tick)
            send_terms(tick)

        @pl.when((tick >= 1) & (tick < KV_HEADS + 1))
        def _():
            sum_and_return(tick - 1)

        @pl.when(tick >= 2)
        def _():
            store(tick - 2)

    for group, heads in enumerate(groups):
        wait_bytes(pieces.at[heads, pl.ds(1, SEGS - 1)], p1_send.at[group])

    @pl.loop(0, KV_HEADS)
    def _(head):
        per_count(
            below, lambda count: wait_bytes(chosen.at[head, pl.ds(0, count)], p3_send.at[head])
        )
        per_count(
            level, lambda count: wait_bytes(terms.at[head, pl.ds(1, count)], b1_send.at[head])
        )

        @pl.when(level < LEVELS - 1)
        def _():
            wait_bytes(final_out.at[head, pl.ds(1, SEGS - 1)], f_send.at[head])


def shards(queries, keys_values, grad_out, parents):
    vmem = pl.BlockSpec(memory_space=pltpu.VMEM)
    smem = pl.BlockSpec(memory_space=pltpu.SMEM)
    anywhere = pl.BlockSpec(memory_space=pl.ANY)
    dma = pltpu.SemaphoreType.DMA
    tile = (SEGS, PIECE, HEAD_DIM)
    keys_count = LEVELS * ROWS
    scratch = [
        pltpu.SMEM((LEVELS, SEGS), jnp.int32),
        pltpu.VMEM((LEVELS, TILE, TILE), BF16),
        pltpu.VMEM((LEVELS, TILE, TILE), BF16),
        pltpu.VMEM(keys_values.shape, BF16),
        pltpu.VMEM(queries.shape, BF16),
        pltpu.VMEM(queries.shape, BF16),
        pltpu.VMEM((KV_HEADS,) + tile, BF16),
        pltpu.VMEM((KV_HEADS,) + tile, BF16),
        pltpu.VMEM((KV_HEADS, LEVELS - 1) + tile, BF16),
        pltpu.VMEM((KV_HEADS, LEVELS) + tile, BF16),
        pltpu.VMEM((KV_HEADS, LEVELS) + tile, BF16),
        pltpu.VMEM((KV_HEADS, LEVELS - 1) + tile, BF16),
        pltpu.VMEM((KV_HEADS, 2, ROWS, HEAD_DIM), F32),
        pltpu.VMEM((2, STACK, HEAD_DIM), BF16),
        pltpu.VMEM((2, HEAD_DIM, STACK), BF16),
        pltpu.VMEM((HEAD_DIM, STACK), F32),
        pltpu.VMEM((3, 8, STACK), F32),
        pltpu.VMEM((keys_count, STACK), F32),
        pltpu.VMEM((keys_count, STACK), F32),
        pltpu.VMEM((PAIR, STACK), BF16),
        pltpu.VMEM((PAIR, STACK), BF16),
        pltpu.VMEM((TILE, HEAD_DIM), F32),
        pltpu.VMEM((KV_HEADS,) + tile, BF16),
        pltpu.VMEM((KV_HEADS,) + tile, BF16),
        dma, dma, dma,
        pltpu.SemaphoreType.REGULAR,
        dma((2,)), dma((2,)),
        dma((KV_HEADS,)), dma((KV_HEADS,)),
        dma((KV_HEADS,)), dma((KV_HEADS,)),
        dma((KV_HEADS,)), dma((KV_HEADS,)),
    ]
    return pl.pallas_call(
        kernel,
        out_shape=(
            jax.ShapeDtypeStruct(queries.shape, BF16),
            jax.ShapeDtypeStruct(keys_values.shape, BF16),
        ),
        in_specs=[smem, anywhere, anywhere, anywhere],
        out_specs=(vmem, vmem),
        scratch_shapes=scratch,
        compiler_params=pltpu.CompilerParams(
            collective_id=0, has_side_effects=True, vmem_limit_bytes=56 * 1024 * 1024
        ),
        cost_estimate=pl.CostEstimate(
            flops=5 * 2 * HEADS * LEVELS * ROWS * ROWS * HEAD_DIM,
            bytes_accessed=8 * 1024 * 1024,
            transcendentals=HEADS * LEVELS * ROWS * ROWS,
        ),
    )(parents.transpose(0, 2, 1), queries, keys_values, grad_out)


def solution(mesh):
    in_specs = (
        P("depth", "seg", None, None),
        P("depth", "seg", None, None, None),
        P("depth", "seg", None, None),
        P(),
    )
    out_specs = (P("depth", "seg", None, None), P("depth", "seg", None, None, None))
    return jax.shard_map(shards, mesh=mesh, in_specs=in_specs, out_specs=out_specs, check_vma=False)
```

profile of v0, /device:TPU:0, one launch (start us, length us, event | category | flops | bytes accessed | tf_op | source)
XLA Modules:
  0.0 82.2 jit_solution(11887464805745343721)
XLA Ops:
  0.6 78.8 %shard_map.59 = (bf16[1,1,128,2560]{3,2,1,0:T(8,128)(2,1)}, bf16[1,1,2,128,512]{4,3,2,1,0:T(8,128)(2,1)}) custom-call(s32[7,1,16]{2,1,0:T(1,128)} %bitcast.1, bf16[1,1,128,2560]{3,2,1,0:T(8,128)(2,1)} %queries.1, bf16[1,1,2,128,512]{4,3,2,1,0:T(8,128)(2,1)} %keys_values.1, bf16[1,1,128,2560]{3,2,1,0:T(8,128)(2,1)} %grad_out.1), custom_call_target="tpu_custom_call" | custom-call | flops 3355443200 | bytes 8388608 | tf_op jit(solution)/shard_map/pallas_call | solution.py:433
  79.5 0.0 copy-start
  79.5 2.0 %copy.8 = bf16[1,1,128,2560]{3,2,1,0:T(8,128)(2,1)} copy(bf16[1,1,128,2560]{3,2,1,0:T(8,128)(2,1)} %get-tuple-element.4) | data formatting | bytes 1310720
  81.5 0.0 copy-done
  81.5 0.7 copy.9
Async XLA Ops:
  79.5 2.0 %copy-start = (bf16[1,1,2,128,512]{4,3,2,1,0:T(8,128)(2,1)S(1)}, bf16[1,1,2,128,512]{4,3,2,1,0:T(8,128)(2,1)}, u32[]{:S(2)}) copy-start(bf16[1,1,2,128,512]{4,3,2,1,0:T(8,128)(2,1)} %get-tuple-element.5) | copy-start | bytes 786436
where the time goes:
time: 82.4 us; the launch traced here: 82.2 us
  Pallas kernels  78.8 us (96%)
  local copies, waits for them, and re-layouts  2.71 us (3%)
    pallas_call x1, Pallas kernels, shards(): pl.pallas_call(kernel, out_shape=(jax.ShapeDtypeStruct(queries.shape, BF1...  78.8 us
    unnamed x4, local copies, waits for them, and re-layouts  2.71 us

commit v1 on v0

--- a/solution.py
+++ b/solution.py
@@ -57,7 +57,7 @@
     parents, queries, keys_values, grad_out, grad_queries, grad_kv,
     anc, pick, spread, kv_in, q_in, g_in, kv_stage, pieces, chosen, blocks,
     terms, term_pieces, own, stacks, turned, query_sum, stats, logits, grad_probs,
-    probs, grad_logits, total_sum, final_out, final_in,
+    probs, grad_logits, final_out, final_in,
     kv_sem, q_sem, g_sem, ready, p1_send, p1_recv, p3_send, p3_recv, b1_send, b1_recv,
     f_send, f_recv,
 ):
@@ -146,24 +146,22 @@
         row = lax.broadcasted_iota(jnp.int32, (PIECE, TILE), 0)
         ahead = lane - row
         for column in range(SEGS):
-            pick[offset, rows_of(column, PIECE), :] = jnp.where(
+            pick[offset - 1, rows_of(column, PIECE), :] = jnp.where(
                 ahead == anc[offset, column] * PIECE, 1.0, 0.0
             ).astype(BF16)
 
     def pick_and_send(head):
-        @pl.loop(1, below + 1)
-        def _(offset):
-            found = jnp.dot(
-                pick[offset], pieces[head].reshape(TILE, HEAD_DIM), preferred_element_type=F32
-            )
-            chosen[head, offset - 1] = found.astype(BF16).reshape(SEGS, PIECE, HEAD_DIM)
-
-        @pl.loop(0, SEGS)
+        found = jnp.dot(
+            pick[...].reshape((LEVELS - 1) * TILE, TILE),
+            pieces[head].reshape(TILE, HEAD_DIM), preferred_element_type=F32,
+        )
+        chosen[head] = found.astype(BF16).reshape(LEVELS - 1, SEGS, PIECE, HEAD_DIM)
+
+        @pl.loop(0, below)
         def _(step):
-            column = wrapped(me + step)
-
-            @pl.loop(1, below + 1)
-            def _(offset):
+            offset = below - step
+            for turn in range(SEGS):
+                column = wrapped(me + turn)
                 remote(
                     chosen.at[head, offset - 1, column], blocks.at[head, offset, me],
                     p3_send.at[head], p3_recv.at[head], (level + offset, column),
@@ -193,15 +191,24 @@
         lane = lax.broadcasted_iota(jnp.int32, (PIECE, TILE), 1)
         row = lax.broadcasted_iota(jnp.int32, (PIECE, TILE), 0)
         lane_column = lane >> 4
+        span = pl.ds(pl.multiple_of((offset - 1) * TILE, TILE), TILE)
         target = (lane & (PIECE - 1)) - row
         for column in range(SEGS):
             target = jnp.where(
                 lane_column == column, target + anc[offset, column] * PIECE, target
             )
         for column in range(SEGS):
-            spread[offset, rows_of(column, PIECE), :] = jnp.where(
+            spread[rows_of(column, PIECE), span] = jnp.where(
                 target == column * PIECE, 1.0, 0.0
             ).astype(BF16)
+
+    @pl.loop(below, LEVELS - 1)
+    def _(index):
+        spread[:, pl.ds(pl.multiple_of(index * TILE, TILE), TILE)] = jnp.zeros(
+            (TILE, TILE), BF16
+        )
+        for head in range(KV_HEADS):
+            term_pieces[head, index] = jnp.zeros((SEGS, PIECE, HEAD_DIM), BF16)
 
     load_q.wait()
     load_g.wait()
@@ -301,12 +308,11 @@
             ).astype(BF16)
 
     def send_terms(head):
-        @pl.loop(0, SEGS)
+        @pl.loop(0, level)
         def _(step):
-            peer = wrapped(me + step)
-
-            @pl.loop(1, level + 1)
-            def _(offset):
+            offset = level - step
+            for turn in range(SEGS):
+                peer = wrapped(me + turn)
                 remote(
                     terms.at[head, offset, peer], term_pieces.at[head, offset - 1, me],
                     b1_send.at[head], b1_recv.at[head], (level - offset, peer),
@@ -321,16 +327,11 @@
                     term_pieces.at[head, pl.ds(0, count)], b1_recv.at[head]
                 ),
             )
-            total_sum[...] = jnp.zeros((TILE, HEAD_DIM), F32)
-
-            @pl.loop(1, below + 1)
-            def _(offset):
-                total_sum[...] += jnp.dot(
-                    spread[offset], term_pieces[head, offset - 1].reshape(TILE, HEAD_DIM),
-                    preferred_element_type=F32,
-                )
-
-            final_out[head] = total_sum[...].astype(BF16).reshape(SEGS, PIECE, HEAD_DIM)
+            total = jnp.dot(
+                spread[...], term_pieces[head].reshape((LEVELS - 1) * TILE, HEAD_DIM),
+                preferred_element_type=F32,
+            )
+            final_out[head] = total.astype(BF16).reshape(SEGS, PIECE, HEAD_DIM)
 
             @pl.loop(1, SEGS)
             def _(step):
@@ -394,14 +395,14 @@
 def shards(queries, keys_values, grad_out, parents):
     vmem = pl.BlockSpec(memory_space=pltpu.VMEM)
     smem = pl.BlockSpec(memory_space=pltpu.SMEM)
-    anywhere = pl.BlockSpec(memory_space=pl.ANY)
+    hbm = pl.BlockSpec(memory_space=pltpu.HBM)
     dma = pltpu.SemaphoreType.DMA
     tile = (SEGS, PIECE, HEAD_DIM)
     keys_count = LEVELS * ROWS
     scratch = [
         pltpu.SMEM((LEVELS, SEGS), jnp.int32),
-        pltpu.VMEM((LEVELS, TILE, TILE), BF16),
-        pltpu.VMEM((LEVELS, TILE, TILE), BF16),
+        pltpu.VMEM((LEVELS - 1, TILE, TILE), BF16),
+        pltpu.VMEM((TILE, (LEVELS - 1) * TILE), BF16),
         pltpu.VMEM(keys_values.shape, BF16),
         pltpu.VMEM(queries.shape, BF16),
         pltpu.VMEM(queries.shape, BF16),
@@ -420,7 +421,6 @@
         pltpu.VMEM((keys_count, STACK), F32),
         pltpu.VMEM((PAIR, STACK), BF16),
         pltpu.VMEM((PAIR, STACK), BF16),
-        pltpu.VMEM((TILE, HEAD_DIM), F32),
         pltpu.VMEM((KV_HEADS,) + tile, BF16),
         pltpu.VMEM((KV_HEADS,) + tile, BF16),
         dma, dma, dma,
@@ -436,11 +436,11 @@
             jax.ShapeDtypeStruct(queries.shape, BF16),
             jax.ShapeDtypeStruct(keys_values.shape, BF16),
         ),
-        in_specs=[smem, anywhere, anywhere, anywhere],
+        in_specs=[smem, hbm, hbm, hbm],
         out_specs=(vmem, vmem),
         scratch_shapes=scratch,
         compiler_params=pltpu.CompilerParams(
-            collective_id=0, has_side_effects=True, vmem_limit_bytes=56 * 1024 * 1024
+            collective_id=0, has_side_effects=True, vmem_limit_bytes=32 * 1024 * 1024
         ),
         cost_estimate=pl.CostEstimate(
             flops=5 * 2 * HEADS * LEVELS * ROWS * ROWS * HEAD_DIM,

time: 82.4 us -> 80.7 us (0.979)
  Pallas kernels: 78.8 us -> 74.3 us
  local copies, waits for them, and re-layouts: 2.71 us -> 5.34 us
    pallas_call x1, Pallas kernels: 78.8 us -> 74.3 us  [shards(): pl.pallas_call(kernel, out_shape=(jax.ShapeDtypeStruct(queries.shape, BF1...]
    unnamed x4 -> x10, local copies, waits for them, and re-layouts: 2.71 us -> 5.34 us
where the time goes in v1:
time: 80.7 us; the launch traced here: 80.3 us
  Pallas kernels  74.3 us (92%)
  local copies, waits for them, and re-layouts  5.34 us (7%)
    pallas_call x1, Pallas kernels, shards(): pl.pallas_call(kernel, out_shape=(jax.ShapeDtypeStruct(queries.shape, BF1...  74.3 us
    unnamed x10, local copies, waits for them, and re-layouts  5.34 us

profile of v1, /device:TPU:0, one launch (start us, length us, event | category | flops | bytes accessed | tf_op | source)
XLA Modules:
  0.0 80.3 jit_solution(7239966329124954638)
XLA Ops:
  0.6 0.0 copy-start
  0.6 1.1 %copy-done = bf16[1,1,128,2560]{3,2,1,0:T(8,128)(2,1)S(1)} copy-done((bf16[1,1,128,2560]{3,2,1,0:T(8,128)(2,1)S(1)}, bf16[1,1,128,2560]{3,2,1,0:T(8,128)(2,1)}, u32[]{:S(2)}) %copy-start) | copy-done | bytes 655384
  1.7 0.0 copy-start.1
  1.7 1.1 %copy-done.1 = bf16[1,1,128,2560]{3,2,1,0:T(8,128)(2,1)S(1)} copy-done((bf16[1,1,128,2560]{3,2,1,0:T(8,128)(2,1)S(1)}, bf16[1,1,128,2560]{3,2,1,0:T(8,128)(2,1)}, u32[]{:S(2)}) %copy-start.1) | copy-done | bytes 655384
  2.8 0.0 copy-start.2
  2.8 0.9 %copy-done.2 = bf16[1,1,2,128,512]{4,3,2,1,0:T(8,128)(2,1)S(1)} copy-done((bf16[1,1,2,128,512]{4,3,2,1,0:T(8,128)(2,1)S(1)}, bf16[1,1,2,128,512]{4,3,2,1,0:T(8,128)(2,1)}, u32[]{:S(2)}) %copy-start.2) | copy-done | bytes 262168
  3.8 0.0 copy-start.3
  3.8 0.7 copy-done.3
  4.4 74.3 %shard_map.59 = (bf16[1,1,128,2560]{3,2,1,0:T(8,128)(2,1)S(1)}, bf16[1,1,2,128,512]{4,3,2,1,0:T(8,128)(2,1)S(1)}) custom-call(s32[7,1,16]{2,1,0:T(1,128)S(1)} %bitcast.1, bf16[1,1,128,2560]{3,2,1,0:T(8,128)(2,1)S(1)} %copy-done, bf16[1,1,2,128,512]{4,3,2,1,0:T(8,128)(2,1)S(1)} %copy-done.2, bf16[1,1,128,2560]{3,2,1,0:T(8,128)(2,1)S(1)} %copy-done.1), custom_call_target="tpu_custom_call" | custom-call | flops 3355443200 | bytes 8388608 | tf_op jit(solution)/shard_map/pallas_call | solution.py:433
  78.7 0.8 %copy.8 = bf16[1,1,128,2560]{3,2,1,0:T(8,128)(2,1)} copy(bf16[1,1,128,2560]{3,2,1,0:T(8,128)(2,1)S(1)} %get-tuple-element.4) | data formatting | bytes 1310720
  79.6 0.7 copy.9
Async XLA Ops:
  0.6 1.1 %copy-start = (bf16[1,1,128,2560]{3,2,1,0:T(8,128)(2,1)S(1)}, bf16[1,1,128,2560]{3,2,1,0:T(8,128)(2,1)}, u32[]{:S(2)}) copy-start(bf16[1,1,128,2560]{3,2,1,0:T(8,128)(2,1)} %queries.1) | copy-start | bytes 1966084
  1.7 1.1 %copy-start.1 = (bf16[1,1,128,2560]{3,2,1,0:T(8,128)(2,1)S(1)}, bf16[1,1,128,2560]{3,2,1,0:T(8,128)(2,1)}, u32[]{:S(2)}) copy-start(bf16[1,1,128,2560]{3,2,1,0:T(8,128)(2,1)} %grad_out.1) | copy-start | bytes 1966084
  2.8 0.9 %copy-start.2 = (bf16[1,1,2,128,512]{4,3,2,1,0:T(8,128)(2,1)S(1)}, bf16[1,1,2,128,512]{4,3,2,1,0:T(8,128)(2,1)}, u32[]{:S(2)}) copy-start(bf16[1,1,2,128,512]{4,3,2,1,0:T(8,128)(2,1)} %keys_values.1) | copy-start | bytes 786436
  3.8 0.7 copy-start.3

commit v2 on v1

--- a/solution.py
+++ b/solution.py
@@ -19,6 +19,7 @@
 STACK = GROUP * ROWS
 PAIR = 2 * ROWS
 TILE = SEGS * PIECE
+OWNERS = SEGS // 2
 
 NEG_FILL = -1e30
 SCALE = HEAD_DIM ** -0.5
@@ -49,6 +50,11 @@
     return pl.ds(pl.multiple_of(index * count, count), count)
 
 
+def owner_column(owner, parity):
+    z = half(owner)
+    return 4 * z + 2 * odd(owner) + odd(z + parity)
+
+
 def fold(tile):
     return tile.reshape(tile.shape[0] // 8, 8, tile.shape[1])
 
@@ -56,7 +62,7 @@
 def kernel(
     parents, queries, keys_values, grad_out, grad_queries, grad_kv,
     anc, pick, spread, kv_in, q_in, g_in, kv_stage, pieces, chosen, blocks,
-    terms, term_pieces, own, stacks, turned, query_sum, stats, logits, grad_probs,
+    terms, term_pieces, own, stacks, turned, query_sum, logits, grad_probs,
     probs, grad_logits, final_out, final_in,
     kv_sem, q_sem, g_sem, ready, p1_send, p1_recv, p3_send, p3_recv, b1_send, b1_recv,
     f_send, f_recv,
@@ -64,6 +70,9 @@
     level = lax.axis_index("depth")
     me = lax.axis_index("seg")
     below = LEVELS - 1 - level
+    my_z, my_x = lax.div(me, 4), lax.rem(me, 4)
+    my_parity = odd(my_z + my_x)
+    my_owner = 2 * my_z + half(my_x)
 
     def remote(src, dst, send_sem, recv_sem, device):
         return pltpu.make_async_remote_copy(
@@ -151,11 +160,16 @@
             ).astype(BF16)
 
     def pick_and_send(head):
-        found = jnp.dot(
-            pick[...].reshape((LEVELS - 1) * TILE, TILE),
-            pieces[head].reshape(TILE, HEAD_DIM), preferred_element_type=F32,
-        )
-        chosen[head] = found.astype(BF16).reshape(LEVELS - 1, SEGS, PIECE, HEAD_DIM)
+        def pick_up(count):
+            found = jnp.dot(
+                pick[0:count].reshape(count * TILE, TILE),
+                pieces[head].reshape(TILE, HEAD_DIM), preferred_element_type=F32,
+            )
+            chosen[head, 0:count] = found.astype(BF16).reshape(count, SEGS, PIECE, HEAD_DIM)
+
+        pl.when((below > 0) & (below <= 2))(lambda: pick_up(2))
+        pl.when((below > 2) & (below <= 4))(lambda: pick_up(4))
+        pl.when(below > 4)(lambda: pick_up(LEVELS - 1))
 
         @pl.loop(0, below)
         def _(step):
@@ -207,143 +221,146 @@
         spread[:, pl.ds(pl.multiple_of(index * TILE, TILE), TILE)] = jnp.zeros(
             (TILE, TILE), BF16
         )
-        for head in range(KV_HEADS):
-            term_pieces[head, index] = jnp.zeros((SEGS, PIECE, HEAD_DIM), BF16)
+        for slot in range(2):
+            term_pieces[slot, index] = jnp.zeros((SEGS, 2, PIECE, HEAD_DIM), BF16)
 
     load_q.wait()
     load_g.wait()
     halves = [pl.ds(part * PIECES_PER_PART, PIECES_PER_PART) for part in range(2)]
 
-    def attend(head):
-        pairs = half(level) + 1
+    def attend(head, pairs):
         span_all = [pl.ds(group * ROWS, ROWS) for group in range(GROUP)]
 
         def block_pair(pair, part):
-            return blocks[head, pl.ds(2 * pair, 2), halves[part]].reshape(PAIR, HEAD_DIM)
-
-        stats[0] = jnp.full((8, STACK), NEG_FILL, F32)
+            return blocks[head, 2 * pair:2 * pair + 2, halves[part]].reshape(PAIR, HEAD_DIM)
+
         for index in range(2):
             for group, span in enumerate(span_all):
                 tile = (q_in, g_in)[index][0, 0, :, lanes(head * GROUP + group)]
                 stacks[index, span, :] = tile
                 turned[index, :, span] = tile.T
-
-        @pl.loop(0, pairs)
-        def _(pair):
-            span_rows = rows_of(pair, PAIR)
-            logits[span_rows, :] = jnp.dot(
-                block_pair(pair, 0), turned[0], preferred_element_type=F32
-            )
-            grad_probs[span_rows, :] = jnp.dot(
-                block_pair(pair, 1), turned[1], preferred_element_type=F32
-            )
-
-            @pl.when(pair == 0)
-            def _():
-                u_row = lax.broadcasted_iota(jnp.int32, (ROWS, ROWS), 0)
-                t_row = lax.broadcasted_iota(jnp.int32, (ROWS, ROWS), 1)
-                for span in span_all:
-                    logits[0:ROWS, span] = jnp.where(
-                        u_row <= t_row, logits[0:ROWS, span], NEG_FILL
-                    )
-
-            @pl.when((pair == pairs - 1) & (odd(level) == 0))
-            def _():
-                logits[rows_of(level + 1, ROWS), :] = jnp.full((ROWS, STACK), NEG_FILL, F32)
-
-            for span in span_all:
-                stats[0, :, span] = jnp.maximum(
-                    stats[0, :, span], fold(logits[span_rows, span]).max(0)
+        u_row = lax.broadcasted_iota(jnp.int32, (ROWS, ROWS), 0)
+        t_row = lax.broadcasted_iota(jnp.int32, (ROWS, ROWS), 1)
+        last_seen = odd(level) == 1
+        best = [jnp.full((8, ROWS), NEG_FILL, F32) for group in range(GROUP)]
+        for pair in range(pairs):
+            raw = jnp.dot(block_pair(pair, 0), turned[0], preferred_element_type=F32)
+            for group, span in enumerate(span_all):
+                first = raw[0:ROWS, group * ROWS:(group + 1) * ROWS]
+                second = raw[ROWS:PAIR, group * ROWS:(group + 1) * ROWS]
+                if pair == 0:
+                    first = jnp.where(u_row <= t_row, first, NEG_FILL)
+                if pair == pairs - 1:
+                    second = jnp.where(last_seen, second, NEG_FILL)
+                logits[pair * PAIR:pair * PAIR + ROWS, span] = first
+                logits[pair * PAIR + ROWS:(pair + 1) * PAIR, span] = second
+                best[group] = jnp.maximum(
+                    best[group], jnp.maximum(fold(first).max(0), fold(second).max(0))
                 )
-
-        stats[1] = jnp.zeros((8, STACK), F32)
-        stats[2] = jnp.zeros((8, STACK), F32)
-        stats[0] = jnp.broadcast_to(stats[0].max(0, keepdims=True), (8, STACK))
-
-        @pl.loop(0, pairs)
-        def _(pair):
-            span_rows = rows_of(pair, PAIR)
-            for span in span_all:
-                top = stats[0, 0:1, span]
-                tile = jnp.exp2((logits[span_rows, span] - top) * EXP2_SCALE)
-                logits[span_rows, span] = tile
-                stats[1, :, span] += fold(tile).sum(0)
-                stats[2, :, span] += fold(tile * grad_probs[span_rows, span]).sum(0)
-
-        inverse = 1.0 / stats[1].sum(0, keepdims=True)
-        delta = stats[2].sum(0, keepdims=True) * inverse
-        stats[1] = jnp.broadcast_to(inverse, (8, STACK))
-        stats[2] = jnp.broadcast_to(delta, (8, STACK))
-        query_sum[...] = jnp.zeros((HEAD_DIM, STACK), F32)
-
-        @pl.loop(0, pairs)
-        def _(pair):
-            span_rows = rows_of(pair, PAIR)
-            for span in span_all:
-                exact = logits[span_rows, span] * stats[1, 0:1, span]
-                probs[:, span] = exact.astype(BF16)
-                grad_logits[:, span] = (
-                    exact * (grad_probs[span_rows, span] - stats[2, 0:1, span])
+        top = [value.max(0, keepdims=True) for value in best]
+        total = [jnp.zeros((8, ROWS), F32) for group in range(GROUP)]
+        delta = [jnp.zeros((8, ROWS), F32) for group in range(GROUP)]
+        for pair in range(pairs):
+            rows = slice(pair * PAIR, (pair + 1) * PAIR)
+            raw = jnp.dot(block_pair(pair, 1), turned[1], preferred_element_type=F32)
+            for group, span in enumerate(span_all):
+                tile = jnp.exp2((logits[rows, span] - top[group]) * EXP2_SCALE)
+                part = raw[:, group * ROWS:(group + 1) * ROWS]
+                logits[rows, span] = tile
+                grad_probs[rows, span] = part
+                total[group] += fold(tile).sum(0)
+                delta[group] += fold(tile * part).sum(0)
+        inverse = [1.0 / value.sum(0, keepdims=True) for value in total]
+        delta = [value.sum(0, keepdims=True) * by for value, by in zip(delta, inverse)]
+        for pair in range(pairs):
+            rows = slice(pair * PAIR, (pair + 1) * PAIR)
+            for group, span in enumerate(span_all):
+                exact = logits[rows, span] * inverse[group]
+                probs[rows, span] = exact.astype(BF16)
+                grad_logits[rows, span] = (
+                    exact * (grad_probs[rows, span] - delta[group])
                 ).astype(BF16)
-            value_term = jnp.dot(probs[...], stacks[1], preferred_element_type=F32)
+            value_term = jnp.dot(probs[rows, :], stacks[1], preferred_element_type=F32)
             key_term = SCALE * jnp.dot(
-                grad_logits[...], stacks[0], preferred_element_type=F32
+                grad_logits[rows, :], stacks[0], preferred_element_type=F32
             )
             for part, term in enumerate((key_term, value_term)):
-                cut = term.astype(BF16).reshape(2, PIECES_PER_PART, PIECE, HEAD_DIM)
-                terms[head, pl.ds(2 * pair, 2), halves[part]] = cut
-
-                @pl.when(pair == 0)
-                def _():
+                terms[head, 2 * pair:2 * pair + 2, halves[part]] = term.astype(BF16).reshape(
+                    2, PIECES_PER_PART, PIECE, HEAD_DIM
+                )
+                if pair == 0:
                     own[head, part] = term[0:ROWS]
-
-            query_sum[...] += lax.dot_general(
-                block_pair(pair, 0), grad_logits[...], (((0,), (0,)), ((), ())),
+            moved = lax.dot_general(
+                block_pair(pair, 0), grad_logits[rows, :], (((0,), (0,)), ((), ())),
                 preferred_element_type=F32,
             )
-
+            if pair == 0:
+                query_sum[...] = moved
+            else:
+                query_sum[...] += moved
         for group, span in enumerate(span_all):
             grad_queries[0, 0, :, lanes(head * GROUP + group)] = (
                 SCALE * query_sum[:, span].T
             ).astype(BF16)
 
     def send_terms(head):
+        targets = []
+        for turn in range(OWNERS):
+            owner = my_owner + turn
+            owner = jnp.where(owner >= OWNERS, owner - OWNERS, owner)
+            targets.append((owner, owner_column(owner, odd(head))))
+
         @pl.loop(0, level)
         def _(step):
             offset = level - step
-            for turn in range(SEGS):
-                peer = wrapped(me + turn)
+            for owner, column in targets:
                 remote(
-                    terms.at[head, offset, peer], term_pieces.at[head, offset - 1, me],
-                    b1_send.at[head], b1_recv.at[head], (level - offset, peer),
+                    terms.at[head, offset, pl.ds(2 * owner, 2)],
+                    term_pieces.at[half(head), offset - 1, me],
+                    b1_send.at[head], b1_recv.at[half(head)], (level - offset, column),
                 ).start()
 
     def sum_and_return(head):
-        @pl.when(level < LEVELS - 1)
+        slot = half(head)
+
+        @pl.when((level < LEVELS - 1) & (odd(head) == my_parity))
         def _():
             per_count(
                 below,
                 lambda count: wait_bytes(
-                    term_pieces.at[head, pl.ds(0, count)], b1_recv.at[head]
+                    term_pieces.at[slot, pl.ds(0, count)], b1_recv.at[slot]
                 ),
             )
-            total = jnp.dot(
-                spread[...], term_pieces[head].reshape((LEVELS - 1) * TILE, HEAD_DIM),
-                preferred_element_type=F32,
-            )
-            final_out[head] = total.astype(BF16).reshape(SEGS, PIECE, HEAD_DIM)
-
-            @pl.loop(1, SEGS)
-            def _(step):
-                peer = wrapped(me + step)
+
+            def add_up(count):
+                received = term_pieces[slot, 0:count]
+                total = jnp.dot(
+                    spread[:, 0:count * TILE],
+                    jnp.concatenate(
+                        [
+                            received[:, :, index].reshape(count * TILE, HEAD_DIM)
+                            for index in range(2)
+                        ],
+                        axis=1,
+                    ),
+                    preferred_element_type=F32,
+                )
+                for index in range(2):
+                    final_out[slot, :, index] = total[
+                        :, index * HEAD_DIM:(index + 1) * HEAD_DIM
+                    ].astype(BF16).reshape(SEGS, PIECE, HEAD_DIM)
+
+            pl.when(below <= 2)(lambda: add_up(2))
+            pl.when((below > 2) & (below <= 4))(lambda: add_up(4))
+            pl.when(below > 4)(lambda: add_up(LEVELS - 1))
+            landing = final_in.at[head, pl.ds(2 * my_owner, 2)]
+            for turn in range(1, SEGS):
+                peer = wrapped(me + turn)
                 remote(
-                    final_out.at[head, peer], final_in.at[head, me],
-                    f_send.at[head], f_recv.at[head], (level, peer),
+                    final_out.at[slot, peer], landing,
+                    f_send.at[slot], f_recv.at[head], (level, peer),
                 ).start()
-
-            pltpu.make_async_copy(
-                final_out.at[head, me], final_in.at[head, me], f_recv.at[head]
-            ).start()
+            pltpu.make_async_copy(final_out.at[slot, me], landing, f_recv.at[head]).start()
 
     def store(head):
         @pl.when(level < LEVELS - 1)
@@ -364,7 +381,8 @@
                 level,
                 lambda count: wait_bytes(blocks.at[tick, pl.ds(1, count)], p3_recv.at[tick]),
             )
-            attend(tick)
+            for pairs in range(1, LEVELS // 2 + 1):
+                pl.when(half(level) == pairs - 1)(functools.partial(attend, tick, pairs))
             send_terms(tick)
 
         @pl.when((tick >= 1) & (tick < KV_HEADS + 1))
@@ -387,9 +405,10 @@
             level, lambda count: wait_bytes(terms.at[head, pl.ds(1, count)], b1_send.at[head])
         )
 
-        @pl.when(level < LEVELS - 1)
-        def _():
-            wait_bytes(final_out.at[head, pl.ds(1, SEGS - 1)], f_send.at[head])
+    @pl.when(level < LEVELS - 1)
+    def _():
+        for slot in range(2):
+            wait_bytes(final_out.at[slot, pl.ds(1, SEGS - 1)], f_send.at[slot])
 
 
 def shards(queries, keys_values, grad_out, parents):
@@ -411,24 +430,23 @@
         pltpu.VMEM((KV_HEADS, LEVELS - 1) + tile, BF16),
         pltpu.VMEM((KV_HEADS, LEVELS) + tile, BF16),
         pltpu.VMEM((KV_HEADS, LEVELS) + tile, BF16),
-        pltpu.VMEM((KV_HEADS, LEVELS - 1) + tile, BF16),
+        pltpu.VMEM((2, LEVELS - 1, SEGS, 2, PIECE, HEAD_DIM), BF16),
         pltpu.VMEM((KV_HEADS, 2, ROWS, HEAD_DIM), F32),
         pltpu.VMEM((2, STACK, HEAD_DIM), BF16),
         pltpu.VMEM((2, HEAD_DIM, STACK), BF16),
         pltpu.VMEM((HEAD_DIM, STACK), F32),
-        pltpu.VMEM((3, 8, STACK), F32),
         pltpu.VMEM((keys_count, STACK), F32),
         pltpu.VMEM((keys_count, STACK), F32),
-        pltpu.VMEM((PAIR, STACK), BF16),
-        pltpu.VMEM((PAIR, STACK), BF16),
-        pltpu.VMEM((KV_HEADS,) + tile, BF16),
+        pltpu.VMEM((keys_count, STACK), BF16),
+        pltpu.VMEM((keys_count, STACK), BF16),
+        pltpu.VMEM((2, SEGS, 2, PIECE, HEAD_DIM), BF16),
         pltpu.VMEM((KV_HEADS,) + tile, BF16),
         dma, dma, dma,
         pltpu.SemaphoreType.REGULAR,
         dma((2,)), dma((2,)),
         dma((KV_HEADS,)), dma((KV_HEADS,)),
-        dma((KV_HEADS,)), dma((KV_HEADS,)),
-        dma((KV_HEADS,)), dma((KV_HEADS,)),
+        dma((KV_HEADS,)), dma((2,)),
+        dma((2,)), dma((KV_HEADS,)),
     ]
     return pl.pallas_call(
         kernel,
@@ -440,7 +458,7 @@
         out_specs=(vmem, vmem),
         scratch_shapes=scratch,
         compiler_params=pltpu.CompilerParams(
-            collective_id=0, has_side_effects=True, vmem_limit_bytes=32 * 1024 * 1024
+            collective_id=0, has_side_effects=True, vmem_limit_bytes=56 * 1024 * 1024
         ),
         cost_estimate=pl.CostEstimate(
             flops=5 * 2 * HEADS * LEVELS * ROWS * ROWS * HEAD_DIM,

time: 80.7 us -> 80.2 us (level)
  local copies, waits for them, and re-layouts: 5.34 us -> 2.71 us
  Pallas kernels: 74.3 us -> 76 us
    unnamed x10 -> x4, local copies, waits for them, and re-layouts: 5.34 us -> 2.71 us
    pallas_call x1, Pallas kernels: 74.3 us -> 76 us  [shards(): pl.pallas_call(kernel, out_shape=(jax.ShapeDtypeStruct(queries.shape, BF1...]
where the time goes in v2:
time: 80.2 us; the launch traced here: 79.3 us
  Pallas kernels  76 us (95%)
  local copies, waits for them, and re-layouts  2.71 us (3%)
    pallas_call x1, Pallas kernels, shards(): pl.pallas_call(kernel, out_shape=(jax.ShapeDtypeStruct(queries.shape, BF1...  76 us
    unnamed x4, local copies, waits for them, and re-layouts  2.71 us

profile of v2, /device:TPU:0, one launch (start us, length us, event | category | flops | bytes accessed | tf_op | source)
XLA Modules:
  0.0 79.3 jit_solution(8236195934827556695)
XLA Ops:
  0.6 76.0 %shard_map.59 = (bf16[1,1,128,2560]{3,2,1,0:T(8,128)(2,1)}, bf16[1,1,2,128,512]{4,3,2,1,0:T(8,128)(2,1)}) custom-call(s32[7,1,16]{2,1,0:T(1,128)} %bitcast.1, bf16[1,1,128,2560]{3,2,1,0:T(8,128)(2,1)} %queries.1, bf16[1,1,2,128,512]{4,3,2,1,0:T(8,128)(2,1)} %keys_values.1, bf16[1,1,128,2560]{3,2,1,0:T(8,128)(2,1)} %grad_out.1), custom_call_target="tpu_custom_call" | custom-call | flops 3355443200 | bytes 8388608 | tf_op jit(solution)/shard_map/pallas_call | solution.py:451
  76.6 0.0 copy-start
  76.6 2.0 %copy.8 = bf16[1,1,128,2560]{3,2,1,0:T(8,128)(2,1)} copy(bf16[1,1,128,2560]{3,2,1,0:T(8,128)(2,1)} %get-tuple-element.4) | data formatting | bytes 1310720
  78.6 0.0 copy-done
  78.6 0.7 copy.9
Async XLA Ops:
  76.6 2.0 %copy-start = (bf16[1,1,2,128,512]{4,3,2,1,0:T(8,128)(2,1)S(1)}, bf16[1,1,2,128,512]{4,3,2,1,0:T(8,128)(2,1)}, u32[]{:S(2)}) copy-start(bf16[1,1,2,128,512]{4,3,2,1,0:T(8,128)(2,1)} %get-tuple-element.5) | copy-start | bytes 786436

commit v3 on v2

--- a/solution.py
+++ b/solution.py
@@ -128,22 +128,26 @@
             ].reshape(PIECES_PER_PART, PIECE, HEAD_DIM)
     pl.semaphore_wait(barrier, SEGS - 1 + LEVELS - 1)
 
-    def spread_out(group, heads):
-        @pl.loop(1, SEGS)
-        def _(step):
-            peer = wrapped(me + step)
-            remote(
-                kv_stage.at[heads, peer], pieces.at[heads, me],
-                p1_send.at[group], p1_recv.at[group], (level, peer),
-            ).start()
-
-        pltpu.make_async_copy(
-            kv_stage.at[heads, me], pieces.at[heads, me], p1_recv.at[group]
-        ).start()
-
-    groups = (pl.ds(0, 1), pl.ds(1, KV_HEADS - 1))
-    for group, heads in enumerate(groups):
-        spread_out(group, heads)
+    def owner_after(turn):
+        owner = my_owner + turn
+        return jnp.where(owner >= OWNERS, owner - OWNERS, owner)
+
+    for slot in range(2):
+        for turn in range(OWNERS):
+            for parity in range(2):
+                owner = owner_after(turn)
+                source = kv_stage.at[2 * slot + parity, pl.ds(2 * owner, 2)]
+                copy = remote(
+                    source, pieces.at[slot, me], p1_send.at[slot], p1_recv.at[slot],
+                    (level, owner_column(owner, parity)),
+                )
+                if turn > 0:
+                    copy.start()
+                else:
+                    pl.when(my_parity != parity)(copy.start)
+                    pl.when(my_parity == parity)(
+                        pltpu.make_async_copy(source, pieces.at[slot, me], p1_recv.at[slot]).start
+                    )
 
     @pl.loop(1, LEVELS)
     def _(step):
@@ -159,13 +163,22 @@
                 ahead == anc[offset, column] * PIECE, 1.0, 0.0
             ).astype(BF16)
 
-    def pick_and_send(head):
+    def pick_and_send(slot):
+        wait_bytes(pieces.at[slot], p1_recv.at[slot])
+        head = 2 * slot + my_parity
+
         def pick_up(count):
             found = jnp.dot(
                 pick[0:count].reshape(count * TILE, TILE),
-                pieces[head].reshape(TILE, HEAD_DIM), preferred_element_type=F32,
-            )
-            chosen[head, 0:count] = found.astype(BF16).reshape(count, SEGS, PIECE, HEAD_DIM)
+                jnp.concatenate(
+                    [pieces[slot, :, index].reshape(TILE, HEAD_DIM) for index in range(2)], axis=1
+                ),
+                preferred_element_type=F32,
+            ).astype(BF16)
+            for index in range(2):
+                chosen[slot, 0:count, :, index] = found[
+                    :, index * HEAD_DIM:(index + 1) * HEAD_DIM
+                ].reshape(count, SEGS, PIECE, HEAD_DIM)
 
         pl.when((below > 0) & (below <= 2))(lambda: pick_up(2))
         pl.when((below > 2) & (below <= 4))(lambda: pick_up(4))
@@ -177,20 +190,13 @@
             for turn in range(SEGS):
                 column = wrapped(me + turn)
                 remote(
-                    chosen.at[head, offset - 1, column], blocks.at[head, offset, me],
-                    p3_send.at[head], p3_recv.at[head], (level + offset, column),
+                    chosen.at[slot, offset - 1, column],
+                    blocks.at[head, offset, pl.ds(2 * my_owner, 2)],
+                    p3_send.at[slot], p3_recv.at[head], (level + offset, column),
                 ).start()
 
-    wait_bytes(pieces.at[groups[0]], p1_recv.at[0])
     pl.semaphore_wait(ready, LEVELS - 1)
-
-    @pl.loop(0, KV_HEADS)
-    def _(head):
-        @pl.when(head == 1)
-        def _():
-            wait_bytes(pieces.at[groups[1]], p1_recv.at[1])
-
-        pick_and_send(head)
+    pl.loop(0, 2)(pick_and_send)
 
     @pl.loop(0, KV_HEADS)
     def _(head):
@@ -306,8 +312,7 @@
     def send_terms(head):
         targets = []
         for turn in range(OWNERS):
-            owner = my_owner + turn
-            owner = jnp.where(owner >= OWNERS, owner - OWNERS, owner)
+            owner = owner_after(turn)
             targets.append((owner, owner_column(owner, odd(head))))
 
         @pl.loop(0, level)
@@ -393,14 +398,17 @@
         def _():
             store(tick - 2)
 
-    for group, heads in enumerate(groups):
-        wait_bytes(pieces.at[heads, pl.ds(1, SEGS - 1)], p1_send.at[group])
+    for slot in range(2):
+        wait_bytes(pieces.at[slot, pl.ds(1, SEGS - 1)], p1_send.at[slot])
+        per_count(
+            below,
+            lambda count, slot=slot: wait_bytes(
+                chosen.at[slot, pl.ds(0, count)], p3_send.at[slot]
+            ),
+        )
 
     @pl.loop(0, KV_HEADS)
     def _(head):
-        per_count(
-            below, lambda count: wait_bytes(chosen.at[head, pl.ds(0, count)], p3_send.at[head])
-        )
         per_count(
             level, lambda count: wait_bytes(terms.at[head, pl.ds(1, count)], b1_send.at[head])
         )
@@ -426,8 +434,8 @@
         pltpu.VMEM(queries.shape, BF16),
         pltpu.VMEM(queries.shape, BF16),
         pltpu.VMEM((KV_HEADS,) + tile, BF16),
-        pltpu.VMEM((KV_HEADS,) + tile, BF16),
-        pltpu.VMEM((KV_HEADS, LEVELS - 1) + tile, BF16),
+        pltpu.VMEM((2, SEGS, 2, PIECE, HEAD_DIM), BF16),
+        pltpu.VMEM((2, LEVELS - 1, SEGS, 2, PIECE, HEAD_DIM), BF16),
         pltpu.VMEM((KV_HEADS, LEVELS) + tile, BF16),
         pltpu.VMEM((KV_HEADS, LEVELS) + tile, BF16),
         pltpu.VMEM((2, LEVELS - 1, SEGS, 2, PIECE, HEAD_DIM), BF16),
@@ -444,7 +452,7 @@
         dma, dma, dma,
         pltpu.SemaphoreType.REGULAR,
         dma((2,)), dma((2,)),
-        dma((KV_HEADS,)), dma((KV_HEADS,)),
+        dma((2,)), dma((KV_HEADS,)),
         dma((KV_HEADS,)), dma((2,)),
         dma((2,)), dma((KV_HEADS,)),
     ]

time: 80.2 us -> 83.8 us (1.045)
  Pallas kernels: 76 us -> 80 us
    pallas_call x1, Pallas kernels: 76 us -> 80 us  [shards(): pl.pallas_call(kernel, out_shape=(jax.ShapeDtypeStruct(queries.shape, BF1...]
where the time goes in v3:
time: 83.8 us; the launch traced here: 83.4 us
  Pallas kernels  80 us (95%)
  local copies, waits for them, and re-layouts  2.71 us (3%)
    pallas_call x1, Pallas kernels, shards(): pl.pallas_call(kernel, out_shape=(jax.ShapeDtypeStruct(queries.shape, BF1...  80 us
    unnamed x4, local copies, waits for them, and re-layouts  2.71 us

profile of v3, /device:TPU:0, one launch (start us, length us, event | category | flops | bytes accessed | tf_op | source)
XLA Modules:
  0.0 83.4 jit_solution(9905029613524403989)
XLA Ops:
  0.6 80.0 %shard_map.59 = (bf16[1,1,128,2560]{3,2,1,0:T(8,128)(2,1)}, bf16[1,1,2,128,512]{4,3,2,1,0:T(8,128)(2,1)}) custom-call(s32[7,1,16]{2,1,0:T(1,128)} %bitcast.1, bf16[1,1,128,2560]{3,2,1,0:T(8,128)(2,1)} %queries.1, bf16[1,1,2,128,512]{4,3,2,1,0:T(8,128)(2,1)} %keys_values.1, bf16[1,1,128,2560]{3,2,1,0:T(8,128)(2,1)} %grad_out.1), custom_call_target="tpu_custom_call" | custom-call | flops 3355443200 | bytes 8388608 | tf_op jit(solution)/shard_map/pallas_call | solution.py:459
  80.6 0.0 copy-start
  80.6 2.0 %copy.8 = bf16[1,1,128,2560]{3,2,1,0:T(8,128)(2,1)} copy(bf16[1,1,128,2560]{3,2,1,0:T(8,128)(2,1)} %get-tuple-element.4) | data formatting | bytes 1310720
  82.7 0.0 copy-done
  82.7 0.7 copy.9
Async XLA Ops:
  80.6 2.0 %copy-start = (bf16[1,1,2,128,512]{4,3,2,1,0:T(8,128)(2,1)S(1)}, bf16[1,1,2,128,512]{4,3,2,1,0:T(8,128)(2,1)}, u32[]{:S(2)}) copy-start(bf16[1,1,2,128,512]{4,3,2,1,0:T(8,128)(2,1)} %get-tuple-element.5) | copy-start | bytes 786436

commit v4 on v3

--- a/solution.py
+++ b/solution.py
@@ -59,13 +59,76 @@
     return tile.reshape(tile.shape[0] // 8, 8, tile.shape[1])
 
 
-def kernel(
-    parents, queries, keys_values, grad_out, grad_queries, grad_kv,
-    anc, pick, spread, kv_in, q_in, g_in, kv_stage, pieces, chosen, blocks,
-    terms, term_pieces, own, stacks, turned, query_sum, logits, grad_probs,
-    probs, grad_logits, final_out, final_in,
-    kv_sem, q_sem, g_sem, ready, p1_send, p1_recv, p3_send, p3_recv, b1_send, b1_recv,
-    f_send, f_recv,
+def remote(src, dst, send_sem, recv_sem, device):
+    return pltpu.make_async_remote_copy(
+        src_ref=src, dst_ref=dst, send_sem=send_sem, recv_sem=recv_sem,
+        device_id=device, device_id_type=MESH,
+    )
+
+
+def wait_bytes(ref, sem):
+    pltpu.make_async_copy(ref, ref, sem).wait()
+
+
+def per_count(which, action):
+    for count in range(1, LEVELS):
+        pl.when(which == count)(functools.partial(action, count))
+
+
+def in_line(level, me, step):
+    other = level + step
+    return (jnp.where(other >= LEVELS, other - LEVELS, other), me)
+
+
+def owner_after(mine, turn):
+    owner = mine + turn
+    return jnp.where(owner >= OWNERS, owner - OWNERS, owner)
+
+
+def greet(level, me):
+    barrier = pltpu.get_barrier_semaphore()
+
+    @pl.loop(1, SEGS)
+    def _(step):
+        pl.semaphore_signal(
+            barrier, inc=1, device_id=(level, wrapped(me + step)), device_id_type=MESH
+        )
+
+    @pl.loop(1, LEVELS)
+    def _(step):
+        pl.semaphore_signal(
+            barrier, inc=1, device_id=in_line(level, me, step), device_id_type=MESH
+        )
+
+
+def greeted():
+    pl.semaphore_wait(pltpu.get_barrier_semaphore(), SEGS - 1 + LEVELS - 1)
+
+
+def pass_word(ready, level, me):
+    @pl.loop(1, LEVELS)
+    def _(step):
+        pl.semaphore_signal(
+            ready, inc=1, device_id=in_line(level, me, step), device_id_type=MESH
+        )
+
+
+def find_columns(parents, anc, level, below):
+    @pl.loop(0, SEGS)
+    def _(column):
+        anc[0, column] = column
+
+    @pl.loop(1, below + 1)
+    def _(offset):
+        @pl.loop(0, SEGS)
+        def _(column):
+            anc[offset, column] = anc[offset - 1, parents[level + offset - 1, 0, column]]
+
+
+def gather_kernel(
+    parents, keys_values, blocks,
+    anc, pick, kv_stage, pieces, chosen,
+    ready, p1_send, p1_recv, p3_send, p3_recv,
 ):
     level = lax.axis_index("depth")
     me = lax.axis_index("seg")
@@ -73,69 +136,19 @@
     my_z, my_x = lax.div(me, 4), lax.rem(me, 4)
     my_parity = odd(my_z + my_x)
     my_owner = 2 * my_z + half(my_x)
-
-    def remote(src, dst, send_sem, recv_sem, device):
-        return pltpu.make_async_remote_copy(
-            src_ref=src, dst_ref=dst, send_sem=send_sem, recv_sem=recv_sem,
-            device_id=device, device_id_type=MESH,
-        )
-
-    def wait_bytes(ref, sem):
-        pltpu.make_async_copy(ref, ref, sem).wait()
-
-    def per_count(which, action):
-        for count in range(1, LEVELS):
-            pl.when(which == count)(functools.partial(action, count))
-
-    load_kv = pltpu.make_async_copy(keys_values, kv_in, kv_sem)
-    load_q = pltpu.make_async_copy(queries, q_in, q_sem)
-    load_g = pltpu.make_async_copy(grad_out, g_in, g_sem)
-    load_kv.start()
-    load_q.start()
-    load_g.start()
-
-    barrier = pltpu.get_barrier_semaphore()
-
-    def in_line(step):
-        other = level + step
-        return (jnp.where(other >= LEVELS, other - LEVELS, other), me)
-
-    @pl.loop(1, SEGS)
-    def _(step):
-        pl.semaphore_signal(
-            barrier, inc=1, device_id=(level, wrapped(me + step)), device_id_type=MESH
-        )
-
-    @pl.loop(1, LEVELS)
-    def _(step):
-        pl.semaphore_signal(barrier, inc=1, device_id=in_line(step), device_id_type=MESH)
-
-    @pl.loop(0, SEGS)
-    def _(column):
-        anc[0, column] = column
-
-    @pl.loop(1, below + 1)
-    def _(offset):
-        @pl.loop(0, SEGS)
-        def _(column):
-            anc[offset, column] = anc[offset - 1, parents[level + offset - 1, 0, column]]
-
-    load_kv.wait()
+    greet(level, me)
+    find_columns(parents, anc, level, below)
     for head in range(KV_HEADS):
         for part in range(2):
-            kv_stage[head, pl.ds(part * PIECES_PER_PART, PIECES_PER_PART)] = kv_in[
+            kv_stage[head, pl.ds(part * PIECES_PER_PART, PIECES_PER_PART)] = keys_values[
                 0, 0, part, :, head * HEAD_DIM:(head + 1) * HEAD_DIM
             ].reshape(PIECES_PER_PART, PIECE, HEAD_DIM)
-    pl.semaphore_wait(barrier, SEGS - 1 + LEVELS - 1)
-
-    def owner_after(turn):
-        owner = my_owner + turn
-        return jnp.where(owner >= OWNERS, owner - OWNERS, owner)
+    greeted()
 
     for slot in range(2):
         for turn in range(OWNERS):
             for parity in range(2):
-                owner = owner_after(turn)
+                owner = owner_after(my_owner, turn)
                 source = kv_stage.at[2 * slot + parity, pl.ds(2 * owner, 2)]
                 copy = remote(
                     source, pieces.at[slot, me], p1_send.at[slot], p1_recv.at[slot],
@@ -149,9 +162,7 @@
                         pltpu.make_async_copy(source, pieces.at[slot, me], p1_recv.at[slot]).start
                     )
 
-    @pl.loop(1, LEVELS)
-    def _(step):
-        pl.semaphore_signal(ready, inc=1, device_id=in_line(step), device_id_type=MESH)
+    pass_word(ready, level, me)
 
     @pl.loop(1, below + 1)
     def _(offset):
@@ -206,32 +217,28 @@
         def _():
             blocks[head, level + 1] = jnp.zeros((SEGS, PIECE, HEAD_DIM), BF16)
 
-    @pl.loop(1, below + 1)
-    def _(offset):
-        lane = lax.broadcasted_iota(jnp.int32, (PIECE, TILE), 1)
-        row = lax.broadcasted_iota(jnp.int32, (PIECE, TILE), 0)
-        lane_column = lane >> 4
-        span = pl.ds(pl.multiple_of((offset - 1) * TILE, TILE), TILE)
-        target = (lane & (PIECE - 1)) - row
-        for column in range(SEGS):
-            target = jnp.where(
-                lane_column == column, target + anc[offset, column] * PIECE, target
-            )
-        for column in range(SEGS):
-            spread[rows_of(column, PIECE), span] = jnp.where(
-                target == column * PIECE, 1.0, 0.0
-            ).astype(BF16)
-
-    @pl.loop(below, LEVELS - 1)
-    def _(index):
-        spread[:, pl.ds(pl.multiple_of(index * TILE, TILE), TILE)] = jnp.zeros(
-            (TILE, TILE), BF16
-        )
-        for slot in range(2):
-            term_pieces[slot, index] = jnp.zeros((SEGS, 2, PIECE, HEAD_DIM), BF16)
-
-    load_q.wait()
-    load_g.wait()
+    for slot in range(2):
+        wait_bytes(pieces.at[slot, pl.ds(1, SEGS - 1)], p1_send.at[slot])
+        per_count(
+            below,
+            lambda count, slot=slot: wait_bytes(
+                chosen.at[slot, pl.ds(0, count)], p3_send.at[slot]
+            ),
+        )
+
+    @pl.loop(0, KV_HEADS)
+    def _(head):
+        per_count(
+            level,
+            lambda count: wait_bytes(blocks.at[head, pl.ds(1, count)], p3_recv.at[head]),
+        )
+
+
+def attend_kernel(
+    blocks, queries, grad_out, grad_queries, terms, own,
+    stacks, turned, query_sum, logits, grad_probs, probs, grad_logits,
+):
+    level = lax.axis_index("depth")
     halves = [pl.ds(part * PIECES_PER_PART, PIECES_PER_PART) for part in range(2)]
 
     def attend(head, pairs):
@@ -242,7 +249,7 @@
 
         for index in range(2):
             for group, span in enumerate(span_all):
-                tile = (q_in, g_in)[index][0, 0, :, lanes(head * GROUP + group)]
+                tile = (queries, grad_out)[index][0, 0, :, lanes(head * GROUP + group)]
                 stacks[index, span, :] = tile
                 turned[index, :, span] = tile.T
         u_row = lax.broadcasted_iota(jnp.int32, (ROWS, ROWS), 0)
@@ -309,10 +316,58 @@
                 SCALE * query_sum[:, span].T
             ).astype(BF16)
 
+    for pairs in range(1, LEVELS // 2 + 1):
+        @pl.when(half(level) == pairs - 1)
+        def _():
+            pl.loop(0, KV_HEADS)(lambda head: attend(head, pairs))
+
+
+def reduce_kernel(
+    parents, terms, own, grad_kv,
+    anc, spread, term_pieces, final_out, final_in,
+    ready, b1_send, b1_recv, f_send, f_recv,
+):
+    level = lax.axis_index("depth")
+    me = lax.axis_index("seg")
+    below = LEVELS - 1 - level
+    my_z, my_x = lax.div(me, 4), lax.rem(me, 4)
+    my_parity = odd(my_z + my_x)
+    my_owner = 2 * my_z + half(my_x)
+    halves = [pl.ds(part * PIECES_PER_PART, PIECES_PER_PART) for part in range(2)]
+    greet(level, me)
+    find_columns(parents, anc, level, below)
+    greeted()
+    pass_word(ready, level, me)
+    @pl.loop(1, below + 1)
+    def _(offset):
+        lane = lax.broadcasted_iota(jnp.int32, (PIECE, TILE), 1)
+        row = lax.broadcasted_iota(jnp.int32, (PIECE, TILE), 0)
+        lane_column = lane >> 4
+        span = pl.ds(pl.multiple_of((offset - 1) * TILE, TILE), TILE)
+        target = (lane & (PIECE - 1)) - row
+        for column in range(SEGS):
+            target = jnp.where(
+                lane_column == column, target + anc[offset, column] * PIECE, target
+            )
+        for column in range(SEGS):
+            spread[rows_of(column, PIECE), span] = jnp.where(
+                target == column * PIECE, 1.0, 0.0
+            ).astype(BF16)
+
+    @pl.loop(below, LEVELS - 1)
+    def _(index):
+        spread[:, pl.ds(pl.multiple_of(index * TILE, TILE), TILE)] = jnp.zeros(
+            (TILE, TILE), BF16
+        )
+        for slot in range(2):
+            term_pieces[slot, index] = jnp.zeros((SEGS, 2, PIECE, HEAD_DIM), BF16)
+
+    pl.semaphore_wait(ready, LEVELS - 1)
+
     def send_terms(head):
         targets = []
         for turn in range(OWNERS):
-            owner = owner_after(turn)
+            owner = owner_after(my_owner, turn)
             targets.append((owner, owner_column(owner, odd(head))))
 
         @pl.loop(0, level)
@@ -372,40 +427,18 @@
         def _():
             wait_bytes(final_in.at[head], f_recv.at[head])
             for part in range(2):
-                own[head, part] += final_in[head, halves[part]].reshape(
-                    ROWS, HEAD_DIM
-                ).astype(F32)
-
-        grad_kv[0, 0, :, :, lanes(head)] = own[head].astype(BF16)
-
-    @pl.loop(0, KV_HEADS + 2)
-    def _(tick):
-        @pl.when(tick < KV_HEADS)
+                grad_kv[0, 0, part, :, lanes(head)] = (
+                    own[head, part]
+                    + final_in[head, halves[part]].reshape(ROWS, HEAD_DIM).astype(F32)
+                ).astype(BF16)
+
+        @pl.when(level == LEVELS - 1)
         def _():
-            per_count(
-                level,
-                lambda count: wait_bytes(blocks.at[tick, pl.ds(1, count)], p3_recv.at[tick]),
-            )
-            for pairs in range(1, LEVELS // 2 + 1):
-                pl.when(half(level) == pairs - 1)(functools.partial(attend, tick, pairs))
-            send_terms(tick)
-
-        @pl.when((tick >= 1) & (tick < KV_HEADS + 1))
-        def _():
-            sum_and_return(tick - 1)
-
-        @pl.when(tick >= 2)
-        def _():
-            store(tick - 2)
-
-    for slot in range(2):
-        wait_bytes(pieces.at[slot, pl.ds(1, SEGS - 1)], p1_send.at[slot])
-        per_count(
-            below,
-            lambda count, slot=slot: wait_bytes(
-                chosen.at[slot, pl.ds(0, count)], p3_send.at[slot]
-            ),
-        )
+            grad_kv[0, 0, :, :, lanes(head)] = own[head].astype(BF16)
+
+    pl.loop(0, KV_HEADS)(send_terms)
+    pl.loop(0, KV_HEADS)(sum_and_return)
+    pl.loop(0, KV_HEADS)(store)
 
     @pl.loop(0, KV_HEADS)
     def _(head):
@@ -422,58 +455,69 @@
 def shards(queries, keys_values, grad_out, parents):
     vmem = pl.BlockSpec(memory_space=pltpu.VMEM)
     smem = pl.BlockSpec(memory_space=pltpu.SMEM)
-    hbm = pl.BlockSpec(memory_space=pltpu.HBM)
     dma = pltpu.SemaphoreType.DMA
+    regular = pltpu.SemaphoreType.REGULAR
     tile = (SEGS, PIECE, HEAD_DIM)
+    double = (SEGS, 2, PIECE, HEAD_DIM)
     keys_count = LEVELS * ROWS
-    scratch = [
-        pltpu.SMEM((LEVELS, SEGS), jnp.int32),
-        pltpu.VMEM((LEVELS - 1, TILE, TILE), BF16),
-        pltpu.VMEM((TILE, (LEVELS - 1) * TILE), BF16),
-        pltpu.VMEM(keys_values.shape, BF16),
-        pltpu.VMEM(queries.shape, BF16),
-        pltpu.VMEM(queries.shape, BF16),
-        pltpu.VMEM((KV_HEADS,) + tile, BF16),
-        pltpu.VMEM((2, SEGS, 2, PIECE, HEAD_DIM), BF16),
-        pltpu.VMEM((2, LEVELS - 1, SEGS, 2, PIECE, HEAD_DIM), BF16),
-        pltpu.VMEM((KV_HEADS, LEVELS) + tile, BF16),
-        pltpu.VMEM((KV_HEADS, LEVELS) + tile, BF16),
-        pltpu.VMEM((2, LEVELS - 1, SEGS, 2, PIECE, HEAD_DIM), BF16),
-        pltpu.VMEM((KV_HEADS, 2, ROWS, HEAD_DIM), F32),
-        pltpu.VMEM((2, STACK, HEAD_DIM), BF16),
-        pltpu.VMEM((2, HEAD_DIM, STACK), BF16),
-        pltpu.VMEM((HEAD_DIM, STACK), F32),
-        pltpu.VMEM((keys_count, STACK), F32),
-        pltpu.VMEM((keys_count, STACK), F32),
-        pltpu.VMEM((keys_count, STACK), BF16),
-        pltpu.VMEM((keys_count, STACK), BF16),
-        pltpu.VMEM((2, SEGS, 2, PIECE, HEAD_DIM), BF16),
-        pltpu.VMEM((KV_HEADS,) + tile, BF16),
-        dma, dma, dma,
-        pltpu.SemaphoreType.REGULAR,
-        dma((2,)), dma((2,)),
-        dma((2,)), dma((KV_HEADS,)),
-        dma((KV_HEADS,)), dma((2,)),
-        dma((2,)), dma((KV_HEADS,)),
-    ]
-    return pl.pallas_call(
-        kernel,
+    found = pltpu.SMEM((LEVELS, SEGS), jnp.int32)
+    all_blocks = jax.ShapeDtypeStruct((KV_HEADS, LEVELS) + tile, BF16)
+    parent_rows = parents.transpose(0, 2, 1)
+
+    def limits(**more):
+        return pltpu.CompilerParams(vmem_limit_bytes=24 * 1024 * 1024, **more)
+
+    blocks = pl.pallas_call(
+        gather_kernel,
+        out_shape=all_blocks,
+        in_specs=[smem, vmem],
+        out_specs=vmem,
+        scratch_shapes=[
+            found,
+            pltpu.VMEM((LEVELS - 1, TILE, TILE), BF16),
+            pltpu.VMEM((KV_HEADS,) + tile, BF16),
+            pltpu.VMEM((2,) + double, BF16),
+            pltpu.VMEM((2, LEVELS - 1) + double, BF16),
+            regular, dma((2,)), dma((2,)), dma((2,)), dma((KV_HEADS,)),
+        ],
+        compiler_params=limits(collective_id=0, has_side_effects=True),
+    )(parent_rows, keys_values)
+    grad_queries, terms, own = pl.pallas_call(
+        attend_kernel,
         out_shape=(
             jax.ShapeDtypeStruct(queries.shape, BF16),
-            jax.ShapeDtypeStruct(keys_values.shape, BF16),
+            all_blocks,
+            jax.ShapeDtypeStruct((KV_HEADS, 2, ROWS, HEAD_DIM), F32),
         ),
-        in_specs=[smem, hbm, hbm, hbm],
-        out_specs=(vmem, vmem),
-        scratch_shapes=scratch,
-        compiler_params=pltpu.CompilerParams(
-            collective_id=0, has_side_effects=True, vmem_limit_bytes=56 * 1024 * 1024
-        ),
-        cost_estimate=pl.CostEstimate(
-            flops=5 * 2 * HEADS * LEVELS * ROWS * ROWS * HEAD_DIM,
-            bytes_accessed=8 * 1024 * 1024,
-            transcendentals=HEADS * LEVELS * ROWS * ROWS,
-        ),
-    )(parents.transpose(0, 2, 1), queries, keys_values, grad_out)
+        in_specs=[vmem, vmem, vmem],
+        out_specs=(vmem, vmem, vmem),
+        scratch_shapes=[
+            pltpu.VMEM((2, STACK, HEAD_DIM), BF16),
+            pltpu.VMEM((2, HEAD_DIM, STACK), BF16),
+            pltpu.VMEM((HEAD_DIM, STACK), F32),
+            pltpu.VMEM((keys_count, STACK), F32),
+            pltpu.VMEM((keys_count, STACK), F32),
+            pltpu.VMEM((keys_count, STACK), BF16),
+            pltpu.VMEM((keys_count, STACK), BF16),
+        ],
+        compiler_params=limits(),
+    )(blocks, queries, grad_out)
+    grad_kv = pl.pallas_call(
+        reduce_kernel,
+        out_shape=jax.ShapeDtypeStruct(keys_values.shape, BF16),
+        in_specs=[smem, vmem, vmem],
+        out_specs=vmem,
+        scratch_shapes=[
+            found,
+            pltpu.VMEM((TILE, (LEVELS - 1) * TILE), BF16),
+            pltpu.VMEM((2, LEVELS - 1) + double, BF16),
+            pltpu.VMEM((2,) + double, BF16),
+            pltpu.VMEM((KV_HEADS,) + tile, BF16),
+            regular, dma((KV_HEADS,)), dma((2,)), dma((2,)), dma((KV_HEADS,)),
+        ],
+        compiler_params=limits(collective_id=1, has_side_effects=True),
+    )(parent_rows, terms, own)
+    return grad_queries, grad_kv
 
 
 def solution(mesh):

time: 83.8 us -> 91.8 us (1.095)
  Pallas kernels: 80 us -> 88.2 us
    pallas_call x1 -> x3, Pallas kernels: 80 us -> 88.2 us  [the longest x1 45.3 us: shards(): pl.pallas_call(reduce_kernel, out_shape=jax.ShapeDtypeStruct(keys_values....]
    unnamed x4 -> x9, local copies, waits for them, and re-layouts: 2.71 us -> 2.44 us
where the time goes in v4:
time: 91.8 us; the launch traced here: 91.3 us
  Pallas kernels  88.2 us (96%)
  local copies, waits for them, and re-layouts  2.44 us (3%)
    pallas_call x1, Pallas kernels, shards(): pl.pallas_call(reduce_kernel, out_shape=jax.ShapeDtypeStruct(keys_values....  45.3 us
    pallas_call x1, Pallas kernels, shards(): pl.pallas_call(gather_kernel, out_shape=all_blocks, in_specs=[smem, vmem]...  37.8 us
    pallas_call x1, Pallas kernels, shards(): pl.pallas_call(attend_kernel, out_shape=(jax.ShapeDtypeStruct(queries.sha...  5.08 us
    unnamed x9, local copies, waits for them, and re-layouts  2.44 us

profile of v4, /device:TPU:0, one launch (start us, length us, event | category | flops | bytes accessed | tf_op | source)
XLA Modules:
  0.0 91.3 jit_solution(16966256354907129425)
XLA Ops:
  0.6 0.0 copy-start.1
  0.6 0.0 copy-start
  0.7 0.0 copy-start.2
  0.7 1.0 %copy-done.2 = bf16[1,1,2,128,512]{4,3,2,1,0:T(8,128)(2,1)S(1)} copy-done((bf16[1,1,2,128,512]{4,3,2,1,0:T(8,128)(2,1)S(1)}, bf16[1,1,2,128,512]{4,3,2,1,0:T(8,128)(2,1)}, u32[]{:S(2)}) %copy-start.2) | copy-done | bytes 262168
  1.7 0.0 copy-start.3
  1.7 0.7 copy-done.3
  2.4 37.8 %shard_map.59.blocks = bf16[4,8,16,16,128]{4,3,2,1,0:T(8,128)(2,1)S(1)} custom-call(s32[7,1,16]{2,1,0:T(1,128)S(1)} %bitcast.1, bf16[1,1,2,128,512]{4,3,2,1,0:T(8,128)(2,1)S(1)} %copy-done.2), custom_call_target="tpu_custom_call" | custom-call | tf_op jit(solution)/shard_map/pallas_call | solution.py:470
  40.2 0.0 copy-done.1
  40.2 0.0 copy-done
  40.2 5.1 %shard_map.60 = (bf16[1,1,128,2560]{3,2,1,0:T(8,128)(2,1)}, bf16[4,8,16,16,128]{4,3,2,1,0:T(8,128)(2,1)S(1)}, f32[4,2,128,128]{3,2,1,0:T(8,128)S(1)}) custom-call(bf16[4,8,16,16,128]{4,3,2,1,0:T(8,128)(2,1)S(1)} %shard_map.59.blocks, bf16[1,1,128,2560]{3,2,1,0:T(8,128)(2,1)S(1)} %copy-done, bf16[1,1,128,2560]{3,2,1,0:T(8,128)(2,1)S(1)} %copy-done.1), custom_call_target="tpu_custom_call" | custom-call | tf_op jit(solution)/shard_map/pallas_call | solution.py:485
  45.3 45.3 %shard_map.61 = bf16[1,1,2,128,512]{4,3,2,1,0:T(8,128)(2,1)S(1)} custom-call(s32[7,1,16]{2,1,0:T(1,128)S(1)} %bitcast.2, bf16[4,8,16,16,128]{4,3,2,1,0:T(8,128)(2,1)S(1)} %get-tuple-element.6.terms, f32[4,2,128,128]{3,2,1,0:T(8,128)S(1)} %get-tuple-element.7.own), custom_call_target="tpu_custom_call" | custom-call | tf_op jit(solution)/shard_map/pallas_call | solution.py:505
  90.6 0.7 copy.7
Async XLA Ops:
  0.6 39.5 %copy-start.1 = (bf16[1,1,128,2560]{3,2,1,0:T(8,128)(2,1)S(1)}, bf16[1,1,128,2560]{3,2,1,0:T(8,128)(2,1)}, u32[]{:S(2)}) copy-start(bf16[1,1,128,2560]{3,2,1,0:T(8,128)(2,1)} %grad_out.1) | copy-start | bytes 1966084
  0.6 39.5 %copy-start = (bf16[1,1,128,2560]{3,2,1,0:T(8,128)(2,1)S(1)}, bf16[1,1,128,2560]{3,2,1,0:T(8,128)(2,1)}, u32[]{:S(2)}) copy-start(bf16[1,1,128,2560]{3,2,1,0:T(8,128)(2,1)} %queries.1) | copy-start | bytes 1966084
  0.7 1.1 %copy-start.2 = (bf16[1,1,2,128,512]{4,3,2,1,0:T(8,128)(2,1)S(1)}, bf16[1,1,2,128,512]{4,3,2,1,0:T(8,128)(2,1)}, u32[]{:S(2)}) copy-start(bf16[1,1,2,128,512]{4,3,2,1,0:T(8,128)(2,1)} %keys_values.1) | copy-start | bytes 786436
  1.7 0.7 copy-start.3

commit v5 on v3

--- a/solution.py
+++ b/solution.py
@@ -132,7 +132,7 @@
         owner = my_owner + turn
         return jnp.where(owner >= OWNERS, owner - OWNERS, owner)
 
-    for slot in range(2):
+    def spread_out(slot):
         for turn in range(OWNERS):
             for parity in range(2):
                 owner = owner_after(turn)
@@ -149,6 +149,8 @@
                         pltpu.make_async_copy(source, pieces.at[slot, me], p1_recv.at[slot]).start
                     )
 
+    spread_out(0)
+
     @pl.loop(1, LEVELS)
     def _(step):
         pl.semaphore_signal(ready, inc=1, device_id=in_line(step), device_id_type=MESH)
@@ -163,8 +165,17 @@
                 ahead == anc[offset, column] * PIECE, 1.0, 0.0
             ).astype(BF16)
 
+    def batch_left(slot, offset):
+        wait_bytes(chosen.at[slot, offset - 1], p3_send.at[slot, offset - 1])
+
+    def last_batches_left(slot):
+        @pl.loop(1, jnp.minimum(below, 2) + 1)
+        def _(offset):
+            batch_left(slot, offset)
+
     def pick_and_send(slot):
         wait_bytes(pieces.at[slot], p1_recv.at[slot])
+        pl.when(slot == 0)(lambda: spread_out(1))
         head = 2 * slot + my_parity
 
         def pick_up(count):
@@ -184,15 +195,19 @@
         pl.when((below > 2) & (below <= 4))(lambda: pick_up(4))
         pl.when(below > 4)(lambda: pick_up(LEVELS - 1))
 
+        pl.when(slot == 1)(lambda: last_batches_left(0))
+
         @pl.loop(0, below)
         def _(step):
             offset = below - step
+            pl.when(step >= 2)(lambda: batch_left(slot, offset + 2))
             for turn in range(SEGS):
                 column = wrapped(me + turn)
                 remote(
                     chosen.at[slot, offset - 1, column],
                     blocks.at[head, offset, pl.ds(2 * my_owner, 2)],
-                    p3_send.at[slot], p3_recv.at[head], (level + offset, column),
+                    p3_send.at[slot, offset - 1], p3_recv.at[head],
+                    (level + offset, column),
                 ).start()
 
     pl.semaphore_wait(ready, LEVELS - 1)
@@ -309,7 +324,13 @@
                 SCALE * query_sum[:, span].T
             ).astype(BF16)
 
+    def terms_left(head):
+        per_count(
+            level, lambda count: wait_bytes(terms.at[head, pl.ds(1, count)], b1_send.at[head])
+        )
+
     def send_terms(head):
+        pl.when(head > 0)(lambda: terms_left(head - 1))
         targets = []
         for turn in range(OWNERS):
             owner = owner_after(turn)
@@ -398,20 +419,10 @@
         def _():
             store(tick - 2)
 
+    last_batches_left(1)
+    terms_left(KV_HEADS - 1)
     for slot in range(2):
         wait_bytes(pieces.at[slot, pl.ds(1, SEGS - 1)], p1_send.at[slot])
-        per_count(
-            below,
-            lambda count, slot=slot: wait_bytes(
-                chosen.at[slot, pl.ds(0, count)], p3_send.at[slot]
-            ),
-        )
-
-    @pl.loop(0, KV_HEADS)
-    def _(head):
-        per_count(
-            level, lambda count: wait_bytes(terms.at[head, pl.ds(1, count)], b1_send.at[head])
-        )
 
     @pl.when(level < LEVELS - 1)
     def _():
@@ -452,7 +463,7 @@
         dma, dma, dma,
         pltpu.SemaphoreType.REGULAR,
         dma((2,)), dma((2,)),
-        dma((2,)), dma((KV_HEADS,)),
+        dma((2, LEVELS - 1)), dma((KV_HEADS,)),
         dma((KV_HEADS,)), dma((2,)),
         dma((2,)), dma((KV_HEADS,)),
     ]

time: 83.8 us -> 80.3 us (0.958)
  Pallas kernels: 80 us -> 76.8 us
    pallas_call x1, Pallas kernels: 80 us -> 76.8 us  [shards(): pl.pallas_call(kernel, out_shape=(jax.ShapeDtypeStruct(queries.shape, BF1...]
where the time goes in v5:
time: 80.3 us; the launch traced here: 80.1 us
  Pallas kernels  76.8 us (96%)
  local copies, waits for them, and re-layouts  2.71 us (3%)
    pallas_call x1, Pallas kernels, shards(): pl.pallas_call(kernel, out_shape=(jax.ShapeDtypeStruct(queries.shape, BF1...  76.8 us
    unnamed x4, local copies, waits for them, and re-layouts  2.71 us

profile of v5, /device:TPU:0, one launch (start us, length us, event | category | flops | bytes accessed | tf_op | source)
XLA Modules:
  0.0 80.1 jit_solution(13657124260163160461)
XLA Ops:
  0.6 76.8 %shard_map.59 = (bf16[1,1,128,2560]{3,2,1,0:T(8,128)(2,1)}, bf16[1,1,2,128,512]{4,3,2,1,0:T(8,128)(2,1)}) custom-call(s32[7,1,16]{2,1,0:T(1,128)} %bitcast.1, bf16[1,1,128,2560]{3,2,1,0:T(8,128)(2,1)} %queries.1, bf16[1,1,2,128,512]{4,3,2,1,0:T(8,128)(2,1)} %keys_values.1, bf16[1,1,128,2560]{3,2,1,0:T(8,128)(2,1)} %grad_out.1), custom_call_target="tpu_custom_call" | custom-call | flops 3355443200 | bytes 8388608 | tf_op jit(solution)/shard_map/pallas_call | solution.py:470
  77.4 0.0 copy-start
  77.4 2.0 %copy.8 = bf16[1,1,128,2560]{3,2,1,0:T(8,128)(2,1)} copy(bf16[1,1,128,2560]{3,2,1,0:T(8,128)(2,1)} %get-tuple-element.4) | data formatting | bytes 1310720
  79.4 0.0 copy-done
  79.4 0.7 copy.9
Async XLA Ops:
  77.4 2.0 %copy-start = (bf16[1,1,2,128,512]{4,3,2,1,0:T(8,128)(2,1)S(1)}, bf16[1,1,2,128,512]{4,3,2,1,0:T(8,128)(2,1)}, u32[]{:S(2)}) copy-start(bf16[1,1,2,128,512]{4,3,2,1,0:T(8,128)(2,1)} %get-tuple-element.5) | copy-start | bytes 786436

commit v6 on v2

--- a/solution.py
+++ b/solution.py
@@ -159,7 +159,13 @@
                 ahead == anc[offset, column] * PIECE, 1.0, 0.0
             ).astype(BF16)
 
+    def batch_left(head, offset):
+        wait_bytes(chosen.at[head, offset - 1], p3_send.at[odd(head), offset - 1])
+
     def pick_and_send(head):
+        pl.when(head == 0)(lambda: wait_bytes(pieces.at[groups[0]], p1_recv.at[0]))
+        pl.when(head == 1)(lambda: wait_bytes(pieces.at[groups[1]], p1_recv.at[1]))
+
         def pick_up(count):
             found = jnp.dot(
                 pick[0:count].reshape(count * TILE, TILE),
@@ -171,26 +177,18 @@
         pl.when((below > 2) & (below <= 4))(lambda: pick_up(4))
         pl.when(below > 4)(lambda: pick_up(LEVELS - 1))
 
-        @pl.loop(0, below)
-        def _(step):
-            offset = below - step
+        @pl.loop(1, below + 1)
+        def _(offset):
+            pl.when(head > 0)(lambda: batch_left(head - 1, offset))
             for turn in range(SEGS):
                 column = wrapped(me + turn)
                 remote(
                     chosen.at[head, offset - 1, column], blocks.at[head, offset, me],
-                    p3_send.at[head], p3_recv.at[head], (level + offset, column),
+                    p3_send.at[odd(head), offset - 1], p3_recv.at[head],
+                    (level + offset, column),
                 ).start()
 
-    wait_bytes(pieces.at[groups[0]], p1_recv.at[0])
     pl.semaphore_wait(ready, LEVELS - 1)
-
-    @pl.loop(0, KV_HEADS)
-    def _(head):
-        @pl.when(head == 1)
-        def _():
-            wait_bytes(pieces.at[groups[1]], p1_recv.at[1])
-
-        pick_and_send(head)
 
     @pl.loop(0, KV_HEADS)
     def _(head):
@@ -200,32 +198,31 @@
         def _():
             blocks[head, level + 1] = jnp.zeros((SEGS, PIECE, HEAD_DIM), BF16)
 
-    @pl.loop(1, below + 1)
-    def _(offset):
-        lane = lax.broadcasted_iota(jnp.int32, (PIECE, TILE), 1)
-        row = lax.broadcasted_iota(jnp.int32, (PIECE, TILE), 0)
-        lane_column = lane >> 4
-        span = pl.ds(pl.multiple_of((offset - 1) * TILE, TILE), TILE)
-        target = (lane & (PIECE - 1)) - row
-        for column in range(SEGS):
-            target = jnp.where(
-                lane_column == column, target + anc[offset, column] * PIECE, target
-            )
-        for column in range(SEGS):
-            spread[rows_of(column, PIECE), span] = jnp.where(
-                target == column * PIECE, 1.0, 0.0
-            ).astype(BF16)
-
-    @pl.loop(below, LEVELS - 1)
-    def _(index):
-        spread[:, pl.ds(pl.multiple_of(index * TILE, TILE), TILE)] = jnp.zeros(
-            (TILE, TILE), BF16
-        )
-        for slot in range(2):
-            term_pieces[slot, index] = jnp.zeros((SEGS, 2, PIECE, HEAD_DIM), BF16)
-
-    load_q.wait()
-    load_g.wait()
+    def make_spread():
+        @pl.loop(1, below + 1)
+        def _(offset):
+            lane = lax.broadcasted_iota(jnp.int32, (PIECE, TILE), 1)
+            row = lax.broadcasted_iota(jnp.int32, (PIECE, TILE), 0)
+            lane_column = lane >> 4
+            span = pl.ds(pl.multiple_of((offset - 1) * TILE, TILE), TILE)
+            target = (lane & (PIECE - 1)) - row
+            for column in range(SEGS):
+                target = jnp.where(
+                    lane_column == column, target + anc[offset, column] * PIECE, target
+                )
+            for column in range(SEGS):
+                spread[rows_of(column, PIECE), span] = jnp.where(
+                    target == column * PIECE, 1.0, 0.0
+                ).astype(BF16)
+
+        @pl.loop(below, LEVELS - 1)
+        def _(index):
+            spread[:, pl.ds(pl.multiple_of(index * TILE, TILE), TILE)] = jnp.zeros(
+                (TILE, TILE), BF16
+            )
+            for slot in range(2):
+                term_pieces[slot, index] = jnp.zeros((SEGS, 2, PIECE, HEAD_DIM), BF16)
+
     halves = [pl.ds(part * PIECES_PER_PART, PIECES_PER_PART) for part in range(2)]
 
     def attend(head, pairs):
@@ -303,6 +300,9 @@
                 SCALE * query_sum[:, span].T
             ).astype(BF16)
 
+    def terms_left(head, offset):
+        wait_bytes(terms.at[head, offset], b1_send.at[odd(head), offset - 1])
+
     def send_terms(head):
         targets = []
         for turn in range(OWNERS):
@@ -310,14 +310,15 @@
             owner = jnp.where(owner >= OWNERS, owner - OWNERS, owner)
             targets.append((owner, owner_column(owner, odd(head))))
 
-        @pl.loop(0, level)
-        def _(step):
-            offset = level - step
+        @pl.loop(1, level + 1)
+        def _(offset):
+            pl.when(head > 0)(lambda: terms_left(head - 1, offset))
             for owner, column in targets:
                 remote(
                     terms.at[head, offset, pl.ds(2 * owner, 2)],
                     term_pieces.at[half(head), offset - 1, me],
-                    b1_send.at[head], b1_recv.at[half(head)], (level - offset, column),
+                    b1_send.at[odd(head), offset - 1], b1_recv.at[half(head)],
+                    (level - offset, column),
                 ).start()
 
     def sum_and_return(head):
@@ -373,37 +374,47 @@
 
         grad_kv[0, 0, :, :, lanes(head)] = own[head].astype(BF16)
 
-    @pl.loop(0, KV_HEADS + 2)
+    @pl.loop(0, KV_HEADS + 4)
     def _(tick):
         @pl.when(tick < KV_HEADS)
         def _():
+            pick_and_send(tick)
+
+        @pl.when(tick == 0)
+        def _():
+            make_spread()
+            load_q.wait()
+            load_g.wait()
+
+        @pl.when((tick >= 1) & (tick < KV_HEADS + 1))
+        def _():
+            head = tick - 1
             per_count(
                 level,
-                lambda count: wait_bytes(blocks.at[tick, pl.ds(1, count)], p3_recv.at[tick]),
+                lambda count: wait_bytes(blocks.at[head, pl.ds(1, count)], p3_recv.at[head]),
             )
             for pairs in range(1, LEVELS // 2 + 1):
-                pl.when(half(level) == pairs - 1)(functools.partial(attend, tick, pairs))
-            send_terms(tick)
-
-        @pl.when((tick >= 1) & (tick < KV_HEADS + 1))
-        def _():
-            sum_and_return(tick - 1)
-
-        @pl.when(tick >= 2)
-        def _():
-            store(tick - 2)
+                pl.when(half(level) == pairs - 1)(functools.partial(attend, head, pairs))
+            send_terms(head)
+
+        @pl.when((tick >= 3) & (tick < KV_HEADS + 3))
+        def _():
+            sum_and_return(tick - 3)
+
+        @pl.when(tick >= 4)
+        def _():
+            store(tick - 4)
 
     for group, heads in enumerate(groups):
         wait_bytes(pieces.at[heads, pl.ds(1, SEGS - 1)], p1_send.at[group])
 
-    @pl.loop(0, KV_HEADS)
-    def _(head):
-        per_count(
-            below, lambda count: wait_bytes(chosen.at[head, pl.ds(0, count)], p3_send.at[head])
-        )
-        per_count(
-            level, lambda count: wait_bytes(terms.at[head, pl.ds(1, count)], b1_send.at[head])
-        )
+    @pl.loop(1, below + 1)
+    def _(offset):
+        batch_left(KV_HEADS - 1, offset)
+
+    @pl.loop(1, level + 1)
+    def _(offset):
+        terms_left(KV_HEADS - 1, offset)
 
     @pl.when(level < LEVELS - 1)
     def _():
@@ -444,8 +455,8 @@
         dma, dma, dma,
         pltpu.SemaphoreType.REGULAR,
         dma((2,)), dma((2,)),
-        dma((KV_HEADS,)), dma((KV_HEADS,)),
-        dma((KV_HEADS,)), dma((2,)),
+        dma((2, LEVELS - 1)), dma((KV_HEADS,)),
+        dma((2, LEVELS - 1)), dma((2,)),
         dma((2,)), dma((KV_HEADS,)),
     ]
     return pl.pallas_call(

time: 80.2 us -> 69.5 us (0.87)
  Pallas kernels: 76 us -> 66 us
    pallas_call x1, Pallas kernels: 76 us -> 66 us  [shards(): pl.pallas_call(kernel, out_shape=(jax.ShapeDtypeStruct(queries.shape, BF1...]
where the time goes in v6:
time: 69.5 us; the launch traced here: 69.3 us
  Pallas kernels  66 us (95%)
  local copies, waits for them, and re-layouts  2.71 us (4%)
    pallas_call x1, Pallas kernels, shards(): pl.pallas_call(kernel, out_shape=(jax.ShapeDtypeStruct(queries.shape, BF1...  66 us
    unnamed x4, local copies, waits for them, and re-layouts  2.71 us

profile of v6, /device:TPU:0, one launch (start us, length us, event | category | flops | bytes accessed | tf_op | source)
XLA Modules:
  0.0 69.3 jit_solution(7578893992452660382)
XLA Ops:
  0.6 66.0 %shard_map.59 = (bf16[1,1,128,2560]{3,2,1,0:T(8,128)(2,1)}, bf16[1,1,2,128,512]{4,3,2,1,0:T(8,128)(2,1)}) custom-call(s32[7,1,16]{2,1,0:T(1,128)} %bitcast.1, bf16[1,1,128,2560]{3,2,1,0:T(8,128)(2,1)} %queries.1, bf16[1,1,2,128,512]{4,3,2,1,0:T(8,128)(2,1)} %keys_values.1, bf16[1,1,128,2560]{3,2,1,0:T(8,128)(2,1)} %grad_out.1), custom_call_target="tpu_custom_call" | custom-call | flops 3355443200 | bytes 8388608 | tf_op jit(solution)/shard_map/pallas_call | solution.py:462
  66.6 0.0 copy-start
  66.6 2.0 %copy.8 = bf16[1,1,128,2560]{3,2,1,0:T(8,128)(2,1)} copy(bf16[1,1,128,2560]{3,2,1,0:T(8,128)(2,1)} %get-tuple-element.4) | data formatting | bytes 1310720
  68.6 0.0 copy-done
  68.6 0.7 %copy.9 = bf16[1,1,2,128,512]{4,3,2,1,0:T(8,128)(2,1)} copy(bf16[1,1,2,128,512]{4,3,2,1,0:T(8,128)(2,1)S(1)} %copy-done) | data formatting | bytes 524288
Async XLA Ops:
  66.6 2.0 %copy-start = (bf16[1,1,2,128,512]{4,3,2,1,0:T(8,128)(2,1)S(1)}, bf16[1,1,2,128,512]{4,3,2,1,0:T(8,128)(2,1)}, u32[]{:S(2)}) copy-start(bf16[1,1,2,128,512]{4,3,2,1,0:T(8,128)(2,1)} %get-tuple-element.5) | copy-start | bytes 786436

commit v7 on v6

--- a/solution.py
+++ b/solution.py
@@ -128,22 +128,18 @@
             ].reshape(PIECES_PER_PART, PIECE, HEAD_DIM)
     pl.semaphore_wait(barrier, SEGS - 1 + LEVELS - 1)
 
-    def spread_out(group, heads):
-        @pl.loop(1, SEGS)
-        def _(step):
-            peer = wrapped(me + step)
+    def spread_out(head):
+        for turn in range(1, SEGS):
+            peer = wrapped(me + turn)
             remote(
-                kv_stage.at[heads, peer], pieces.at[heads, me],
-                p1_send.at[group], p1_recv.at[group], (level, peer),
+                kv_stage.at[head, peer], pieces.at[head, me],
+                p1_send.at[head], p1_recv.at[head], (level, peer),
             ).start()
-
         pltpu.make_async_copy(
-            kv_stage.at[heads, me], pieces.at[heads, me], p1_recv.at[group]
+            kv_stage.at[head, me], pieces.at[head, me], p1_recv.at[head]
         ).start()
 
-    groups = (pl.ds(0, 1), pl.ds(1, KV_HEADS - 1))
-    for group, heads in enumerate(groups):
-        spread_out(group, heads)
+    spread_out(0)
 
     @pl.loop(1, LEVELS)
     def _(step):
@@ -163,22 +159,17 @@
         wait_bytes(chosen.at[head, offset - 1], p3_send.at[odd(head), offset - 1])
 
     def pick_and_send(head):
-        pl.when(head == 0)(lambda: wait_bytes(pieces.at[groups[0]], p1_recv.at[0]))
-        pl.when(head == 1)(lambda: wait_bytes(pieces.at[groups[1]], p1_recv.at[1]))
-
-        def pick_up(count):
+        wait_bytes(pieces.at[head], p1_recv.at[head])
+        pl.when(head < KV_HEADS - 1)(lambda: spread_out(head + 1))
+
+        @pl.loop(1, below + 1)
+        def _(step):
+            offset = jnp.where(head == 0, below + 1 - step, step)
             found = jnp.dot(
-                pick[0:count].reshape(count * TILE, TILE),
-                pieces[head].reshape(TILE, HEAD_DIM), preferred_element_type=F32,
-            )
-            chosen[head, 0:count] = found.astype(BF16).reshape(count, SEGS, PIECE, HEAD_DIM)
-
-        pl.when((below > 0) & (below <= 2))(lambda: pick_up(2))
-        pl.when((below > 2) & (below <= 4))(lambda: pick_up(4))
-        pl.when(below > 4)(lambda: pick_up(LEVELS - 1))
-
-        @pl.loop(1, below + 1)
-        def _(offset):
+                pick[offset - 1], pieces[head].reshape(TILE, HEAD_DIM),
+                preferred_element_type=F32,
+            )
+            chosen[head, offset - 1] = found.astype(BF16).reshape(SEGS, PIECE, HEAD_DIM)
             pl.when(head > 0)(lambda: batch_left(head - 1, offset))
             for turn in range(SEGS):
                 column = wrapped(me + turn)
@@ -386,6 +377,14 @@
             load_q.wait()
             load_g.wait()
 
+        @pl.when((tick >= 3) & (tick < KV_HEADS + 3))
+        def _():
+            sum_and_return(tick - 3)
+
+        @pl.when(tick >= 4)
+        def _():
+            store(tick - 4)
+
         @pl.when((tick >= 1) & (tick < KV_HEADS + 1))
         def _():
             head = tick - 1
@@ -397,16 +396,9 @@
                 pl.when(half(level) == pairs - 1)(functools.partial(attend, head, pairs))
             send_terms(head)
 
-        @pl.when((tick >= 3) & (tick < KV_HEADS + 3))
-        def _():
-            sum_and_return(tick - 3)
-
-        @pl.when(tick >= 4)
-        def _():
-            store(tick - 4)
-
-    for group, heads in enumerate(groups):
-        wait_bytes(pieces.at[heads, pl.ds(1, SEGS - 1)], p1_send.at[group])
+    @pl.loop(0, KV_HEADS)
+    def _(head):
+        wait_bytes(pieces.at[head, pl.ds(1, SEGS - 1)], p1_send.at[head])
 
     @pl.loop(1, below + 1)
     def _(offset):
@@ -454,7 +446,7 @@
         pltpu.VMEM((KV_HEADS,) + tile, BF16),
         dma, dma, dma,
         pltpu.SemaphoreType.REGULAR,
-        dma((2,)), dma((2,)),
+        dma((KV_HEADS,)), dma((KV_HEADS,)),
         dma((2, LEVELS - 1)), dma((KV_HEADS,)),
         dma((2, LEVELS - 1)), dma((2,)),
         dma((2,)), dma((KV_HEADS,)),

time: 69.5 us -> 68.7 us (0.988)
  Pallas kernels: 66 us -> 65.2 us
    pallas_call x1, Pallas kernels: 66 us -> 65.2 us  [shards(): pl.pallas_call(kernel, out_shape=(jax.ShapeDtypeStruct(queries.shape, BF1...]
where the time goes in v7:
time: 68.7 us; the launch traced here: 68.5 us
  Pallas kernels  65.2 us (95%)
  local copies, waits for them, and re-layouts  2.71 us (4%)
    pallas_call x1, Pallas kernels, shards(): pl.pallas_call(kernel, out_shape=(jax.ShapeDtypeStruct(queries.shape, BF1...  65.2 us
    unnamed x4, local copies, waits for them, and re-layouts  2.71 us

profile of v7, /device:TPU:0, one launch (start us, length us, event | category | flops | bytes accessed | tf_op | source)
XLA Modules:
  0.0 68.5 jit_solution(16730466660366207378)
XLA Ops:
  0.6 65.2 %shard_map.59 = (bf16[1,1,128,2560]{3,2,1,0:T(8,128)(2,1)}, bf16[1,1,2,128,512]{4,3,2,1,0:T(8,128)(2,1)}) custom-call(s32[7,1,16]{2,1,0:T(1,128)} %bitcast.1, bf16[1,1,128,2560]{3,2,1,0:T(8,128)(2,1)} %queries.1, bf16[1,1,2,128,512]{4,3,2,1,0:T(8,128)(2,1)} %keys_values.1, bf16[1,1,128,2560]{3,2,1,0:T(8,128)(2,1)} %grad_out.1), custom_call_target="tpu_custom_call" | custom-call | flops 3355443200 | bytes 8388608 | tf_op jit(solution)/shard_map/pallas_call | solution.py:454
  65.8 0.0 copy-start
  65.8 2.0 %copy.8 = bf16[1,1,128,2560]{3,2,1,0:T(8,128)(2,1)} copy(bf16[1,1,128,2560]{3,2,1,0:T(8,128)(2,1)} %get-tuple-element.4) | data formatting | bytes 1310720
  67.8 0.0 copy-done
  67.8 0.7 %copy.9 = bf16[1,1,2,128,512]{4,3,2,1,0:T(8,128)(2,1)} copy(bf16[1,1,2,128,512]{4,3,2,1,0:T(8,128)(2,1)S(1)} %copy-done) | data formatting | bytes 524288
Async XLA Ops:
  65.8 2.0 %copy-start = (bf16[1,1,2,128,512]{4,3,2,1,0:T(8,128)(2,1)S(1)}, bf16[1,1,2,128,512]{4,3,2,1,0:T(8,128)(2,1)}, u32[]{:S(2)}) copy-start(bf16[1,1,2,128,512]{4,3,2,1,0:T(8,128)(2,1)} %get-tuple-element.5) | copy-start | bytes 786436

commit v8 on v7

--- a/solution.py
+++ b/solution.py
@@ -365,7 +365,9 @@
 
         grad_kv[0, 0, :, :, lanes(head)] = own[head].astype(BF16)
 
-    @pl.loop(0, KV_HEADS + 4)
+    lag = jnp.where(level <= 2, KV_HEADS, 1)
+
+    @pl.loop(0, KV_HEADS + lag + 3)
     def _(tick):
         @pl.when(tick < KV_HEADS)
         def _():
@@ -373,21 +375,16 @@
 
         @pl.when(tick == 0)
         def _():
-            make_spread()
             load_q.wait()
             load_g.wait()
 
-        @pl.when((tick >= 3) & (tick < KV_HEADS + 3))
-        def _():
-            sum_and_return(tick - 3)
-
-        @pl.when(tick >= 4)
-        def _():
-            store(tick - 4)
-
-        @pl.when((tick >= 1) & (tick < KV_HEADS + 1))
-        def _():
-            head = tick - 1
+        @pl.when(tick == KV_HEADS - 1)
+        def _():
+            make_spread()
+
+        @pl.when((tick >= lag) & (tick < KV_HEADS + lag))
+        def _():
+            head = tick - lag
             per_count(
                 level,
                 lambda count: wait_bytes(blocks.at[head, pl.ds(1, count)], p3_recv.at[head]),
@@ -395,6 +392,14 @@
             for pairs in range(1, LEVELS // 2 + 1):
                 pl.when(half(level) == pairs - 1)(functools.partial(attend, head, pairs))
             send_terms(head)
+
+        @pl.when((tick >= lag + 2) & (tick < KV_HEADS + lag + 2))
+        def _():
+            sum_and_return(tick - lag - 2)
+
+        @pl.when(tick >= lag + 3)
+        def _():
+            store(tick - lag - 3)
 
     @pl.loop(0, KV_HEADS)
     def _(head):

time: 68.7 us -> 69.5 us (1.012)
  Pallas kernels: 65.2 us -> 66 us
    pallas_call x1, Pallas kernels: 65.2 us -> 66 us  [shards(): pl.pallas_call(kernel, out_shape=(jax.ShapeDtypeStruct(queries.shape, BF1...]
where the time goes in v8:
time: 69.5 us; the launch traced here: 69.3 us
  Pallas kernels  66 us (95%)
  local copies, waits for them, and re-layouts  2.71 us (4%)
    pallas_call x1, Pallas kernels, shards(): pl.pallas_call(kernel, out_shape=(jax.ShapeDtypeStruct(queries.shape, BF1...  66 us
    unnamed x4, local copies, waits for them, and re-layouts  2.71 us

profile of v8, /device:TPU:0, one launch (start us, length us, event | category | flops | bytes accessed | tf_op | source)
XLA Modules:
  0.0 69.3 jit_solution(9721150151030089990)
XLA Ops:
  0.6 66.0 %shard_map.59 = (bf16[1,1,128,2560]{3,2,1,0:T(8,128)(2,1)}, bf16[1,1,2,128,512]{4,3,2,1,0:T(8,128)(2,1)}) custom-call(s32[7,1,16]{2,1,0:T(1,128)} %bitcast.1, bf16[1,1,128,2560]{3,2,1,0:T(8,128)(2,1)} %queries.1, bf16[1,1,2,128,512]{4,3,2,1,0:T(8,128)(2,1)} %keys_values.1, bf16[1,1,128,2560]{3,2,1,0:T(8,128)(2,1)} %grad_out.1), custom_call_target="tpu_custom_call" | custom-call | flops 3355443200 | bytes 8388608 | tf_op jit(solution)/shard_map/pallas_call | solution.py:459
  66.6 0.0 copy-start
  66.6 2.0 %copy.8 = bf16[1,1,128,2560]{3,2,1,0:T(8,128)(2,1)} copy(bf16[1,1,128,2560]{3,2,1,0:T(8,128)(2,1)} %get-tuple-element.4) | data formatting | bytes 1310720
  68.6 0.0 copy-done
  68.6 0.7 %copy.9 = bf16[1,1,2,128,512]{4,3,2,1,0:T(8,128)(2,1)} copy(bf16[1,1,2,128,512]{4,3,2,1,0:T(8,128)(2,1)S(1)} %copy-done) | data formatting | bytes 524288
Async XLA Ops:
  66.6 2.0 %copy-start = (bf16[1,1,2,128,512]{4,3,2,1,0:T(8,128)(2,1)S(1)}, bf16[1,1,2,128,512]{4,3,2,1,0:T(8,128)(2,1)}, u32[]{:S(2)}) copy-start(bf16[1,1,2,128,512]{4,3,2,1,0:T(8,128)(2,1)} %get-tuple-element.5) | copy-start | bytes 786436

commit v9 on v7

--- a/solution.py
+++ b/solution.py
@@ -70,6 +70,7 @@
     level = lax.axis_index("depth")
     me = lax.axis_index("seg")
     below = LEVELS - 1 - level
+    mirror = LEVELS - 1 - level
     my_z, my_x = lax.div(me, 4), lax.rem(me, 4)
     my_parity = odd(my_z + my_x)
     my_owner = 2 * my_z + half(my_x)
@@ -106,19 +107,27 @@
             barrier, inc=1, device_id=(level, wrapped(me + step)), device_id_type=MESH
         )
 
+        pl.semaphore_signal(
+            barrier, inc=1, device_id=(mirror, wrapped(me + step)), device_id_type=MESH
+        )
+
     @pl.loop(1, LEVELS)
     def _(step):
         pl.semaphore_signal(barrier, inc=1, device_id=in_line(step), device_id_type=MESH)
 
-    @pl.loop(0, SEGS)
-    def _(column):
-        anc[0, column] = column
-
-    @pl.loop(1, below + 1)
-    def _(offset):
+    served = (mirror, level)
+    for index, base in enumerate(served):
         @pl.loop(0, SEGS)
         def _(column):
-            anc[offset, column] = anc[offset - 1, parents[level + offset - 1, 0, column]]
+            anc[index, 0, column] = column
+
+        @pl.loop(1, LEVELS - base)
+        def _(offset):
+            @pl.loop(0, SEGS)
+            def _(column):
+                anc[index, offset, column] = anc[
+                    index, offset - 1, parents[base + offset - 1, 0, column]
+                ]
 
     load_kv.wait()
     for head in range(KV_HEADS):
@@ -126,58 +135,77 @@
             kv_stage[head, pl.ds(part * PIECES_PER_PART, PIECES_PER_PART)] = kv_in[
                 0, 0, part, :, head * HEAD_DIM:(head + 1) * HEAD_DIM
             ].reshape(PIECES_PER_PART, PIECE, HEAD_DIM)
-    pl.semaphore_wait(barrier, SEGS - 1 + LEVELS - 1)
+    pl.semaphore_wait(barrier, 2 * (SEGS - 1) + LEVELS - 1)
 
     def spread_out(head):
+        host = jnp.where(head == 0, mirror, level)
+
+        def copy_to(peer):
+            return remote(
+                kv_stage.at[head, peer], pieces.at[head, me],
+                p1_send.at[head], p1_recv.at[head], (host, peer),
+            )
+
         for turn in range(1, SEGS):
-            peer = wrapped(me + turn)
-            remote(
-                kv_stage.at[head, peer], pieces.at[head, me],
-                p1_send.at[head], p1_recv.at[head], (level, peer),
+            copy_to(wrapped(me + turn)).start()
+        pl.when(head == 0)(lambda: copy_to(me).start())
+        pl.when(head > 0)(
+            lambda: pltpu.make_async_copy(
+                kv_stage.at[head, me], pieces.at[head, me], p1_recv.at[head]
             ).start()
-        pltpu.make_async_copy(
-            kv_stage.at[head, me], pieces.at[head, me], p1_recv.at[head]
-        ).start()
-
-    spread_out(0)
+        )
+
+    pl.loop(0, 2)(spread_out)
 
     @pl.loop(1, LEVELS)
     def _(step):
         pl.semaphore_signal(ready, inc=1, device_id=in_line(step), device_id_type=MESH)
 
-    @pl.loop(1, below + 1)
-    def _(offset):
-        lane = lax.broadcasted_iota(jnp.int32, (PIECE, TILE), 1)
-        row = lax.broadcasted_iota(jnp.int32, (PIECE, TILE), 0)
-        ahead = lane - row
-        for column in range(SEGS):
-            pick[offset - 1, rows_of(column, PIECE), :] = jnp.where(
-                ahead == anc[offset, column] * PIECE, 1.0, 0.0
-            ).astype(BF16)
+    for index, base in enumerate(served):
+        @pl.loop(1, LEVELS - base)
+        def _(offset):
+            lane = lax.broadcasted_iota(jnp.int32, (PIECE, TILE), 1)
+            row = lax.broadcasted_iota(jnp.int32, (PIECE, TILE), 0)
+            ahead = lane - row
+            for column in range(SEGS):
+                pick[index, offset - 1, rows_of(column, PIECE), :] = jnp.where(
+                    ahead == anc[index, offset, column] * PIECE, 1.0, 0.0
+                ).astype(BF16)
 
     def batch_left(head, offset):
-        wait_bytes(chosen.at[head, offset - 1], p3_send.at[odd(head), offset - 1])
+        wait_bytes(chosen.at[head, offset - 1], p3_send.at[head, offset - 1])
 
     def pick_and_send(head):
         wait_bytes(pieces.at[head], p1_recv.at[head])
-        pl.when(head < KV_HEADS - 1)(lambda: spread_out(head + 1))
-
-        @pl.loop(1, below + 1)
-        def _(step):
-            offset = jnp.where(head == 0, below + 1 - step, step)
+        pl.when((head > 0) & (head < KV_HEADS - 1))(lambda: spread_out(head + 1))
+        base = jnp.where(head == 0, mirror, level)
+        index = jnp.where(head == 0, 0, 1)
+
+        @pl.loop(1, LEVELS - base)
+        def _(offset):
             found = jnp.dot(
-                pick[offset - 1], pieces[head].reshape(TILE, HEAD_DIM),
+                pick[index, offset - 1], pieces[head].reshape(TILE, HEAD_DIM),
                 preferred_element_type=F32,
             )
             chosen[head, offset - 1] = found.astype(BF16).reshape(SEGS, PIECE, HEAD_DIM)
-            pl.when(head > 0)(lambda: batch_left(head - 1, offset))
-            for turn in range(SEGS):
-                column = wrapped(me + turn)
-                remote(
+            pl.when(head > 1)(lambda: batch_left(head - 1, offset))
+            target = base + offset
+
+            def copy_to(column):
+                return remote(
                     chosen.at[head, offset - 1, column], blocks.at[head, offset, me],
-                    p3_send.at[odd(head), offset - 1], p3_recv.at[head],
-                    (level + offset, column),
+                    p3_send.at[head, offset - 1], p3_recv.at[head], (target, column),
+                )
+
+            for turn in range(1, SEGS):
+                copy_to(wrapped(me + turn)).start()
+            pl.when(target != level)(lambda: copy_to(me).start())
+            pl.when(target == level)(
+                lambda: pltpu.make_async_copy(
+                    chosen.at[head, offset - 1, me], blocks.at[head, offset, me],
+                    p3_recv.at[head],
                 ).start()
+            )
 
     pl.semaphore_wait(ready, LEVELS - 1)
 
@@ -199,7 +227,7 @@
             target = (lane & (PIECE - 1)) - row
             for column in range(SEGS):
                 target = jnp.where(
-                    lane_column == column, target + anc[offset, column] * PIECE, target
+                    lane_column == column, target + anc[1, offset, column] * PIECE, target
                 )
             for column in range(SEGS):
                 spread[rows_of(column, PIECE), span] = jnp.where(
@@ -367,9 +395,8 @@
 
     @pl.loop(0, KV_HEADS + 4)
     def _(tick):
-        @pl.when(tick < KV_HEADS)
-        def _():
-            pick_and_send(tick)
+        pl.when(tick == 0)(lambda: pick_and_send(0))
+        pl.when(tick < KV_HEADS - 1)(lambda: pick_and_send(tick + 1))
 
         @pl.when(tick == 0)
         def _():
@@ -399,6 +426,14 @@
     @pl.loop(0, KV_HEADS)
     def _(head):
         wait_bytes(pieces.at[head, pl.ds(1, SEGS - 1)], p1_send.at[head])
+        pl.when(head == 0)(lambda: wait_bytes(pieces.at[0, 0], p1_send.at[0]))
+
+    @pl.loop(1, LEVELS - mirror)
+    def _(offset):
+        wait_bytes(chosen.at[0, offset - 1, pl.ds(1, SEGS - 1)], p3_send.at[0, offset - 1])
+        pl.when(mirror + offset != level)(
+            lambda: wait_bytes(chosen.at[0, offset - 1, 0], p3_send.at[0, offset - 1])
+        )
 
     @pl.loop(1, below + 1)
     def _(offset):
@@ -422,8 +457,8 @@
     tile = (SEGS, PIECE, HEAD_DIM)
     keys_count = LEVELS * ROWS
     scratch = [
-        pltpu.SMEM((LEVELS, SEGS), jnp.int32),
-        pltpu.VMEM((LEVELS - 1, TILE, TILE), BF16),
+        pltpu.SMEM((2, LEVELS, SEGS), jnp.int32),
+        pltpu.VMEM((2, LEVELS - 1, TILE, TILE), BF16),
         pltpu.VMEM((TILE, (LEVELS - 1) * TILE), BF16),
         pltpu.VMEM(keys_values.shape, BF16),
         pltpu.VMEM(queries.shape, BF16),
@@ -447,7 +482,7 @@
         dma, dma, dma,
         pltpu.SemaphoreType.REGULAR,
         dma((KV_HEADS,)), dma((KV_HEADS,)),
-        dma((2, LEVELS - 1)), dma((KV_HEADS,)),
+        dma((KV_HEADS, LEVELS - 1)), dma((KV_HEADS,)),
         dma((2, LEVELS - 1)), dma((2,)),
         dma((2,)), dma((KV_HEADS,)),
     ]

time: 68.7 us -> 74.7 us (1.087)
  Pallas kernels: 65.2 us -> 71.1 us
    pallas_call x1, Pallas kernels: 65.2 us -> 71.1 us  [shards(): pl.pallas_call(kernel, out_shape=(jax.ShapeDtypeStruct(queries.shape, BF1...]
where the time goes in v9:
time: 74.7 us; the launch traced here: 74.5 us
  Pallas kernels  71.1 us (95%)
  local copies, waits for them, and re-layouts  2.71 us (4%)
    pallas_call x1, Pallas kernels, shards(): pl.pallas_call(kernel, out_shape=(jax.ShapeDtypeStruct(queries.shape, BF1...  71.1 us
    unnamed x4, local copies, waits for them, and re-layouts  2.71 us

profile of v9, /device:TPU:0, one launch (start us, length us, event | category | flops | bytes accessed | tf_op | source)
XLA Modules:
  0.0 74.5 jit_solution(16357782751913819019)
XLA Ops:
  0.6 71.1 %shard_map.59 = (bf16[1,1,128,2560]{3,2,1,0:T(8,128)(2,1)}, bf16[1,1,2,128,512]{4,3,2,1,0:T(8,128)(2,1)}) custom-call(s32[7,1,16]{2,1,0:T(1,128)} %bitcast.1, bf16[1,1,128,2560]{3,2,1,0:T(8,128)(2,1)} %queries.1, bf16[1,1,2,128,512]{4,3,2,1,0:T(8,128)(2,1)} %keys_values.1, bf16[1,1,128,2560]{3,2,1,0:T(8,128)(2,1)} %grad_out.1), custom_call_target="tpu_custom_call" | custom-call | flops 3355443200 | bytes 8388608 | tf_op jit(solution)/shard_map/pallas_call | solution.py:489
  71.8 0.0 copy-start
  71.8 2.0 %copy.8 = bf16[1,1,128,2560]{3,2,1,0:T(8,128)(2,1)} copy(bf16[1,1,128,2560]{3,2,1,0:T(8,128)(2,1)} %get-tuple-element.4) | data formatting | bytes 1310720
  73.8 0.0 copy-done
  73.8 0.7 copy.9
Async XLA Ops:
  71.8 2.0 %copy-start = (bf16[1,1,2,128,512]{4,3,2,1,0:T(8,128)(2,1)S(1)}, bf16[1,1,2,128,512]{4,3,2,1,0:T(8,128)(2,1)}, u32[]{:S(2)}) copy-start(bf16[1,1,2,128,512]{4,3,2,1,0:T(8,128)(2,1)} %get-tuple-element.5) | copy-start | bytes 786436

commit v10 on v7

--- a/solution.py
+++ b/solution.py
@@ -63,9 +63,9 @@
     parents, queries, keys_values, grad_out, grad_queries, grad_kv,
     anc, pick, spread, kv_in, q_in, g_in, kv_stage, pieces, chosen, blocks,
     terms, term_pieces, own, stacks, turned, query_sum, logits, grad_probs,
-    probs, grad_logits, final_out, final_in,
+    probs, grad_logits, total, final_out, final_in, q_out, kv_out,
     kv_sem, q_sem, g_sem, ready, p1_send, p1_recv, p3_send, p3_recv, b1_send, b1_recv,
-    f_send, f_recv,
+    f_send, f_recv, q_out_sem, kv_out_sem,
 ):
     level = lax.axis_index("depth")
     me = lax.axis_index("seg")
@@ -206,15 +206,18 @@
                     target == column * PIECE, 1.0, 0.0
                 ).astype(BF16)
 
-        @pl.loop(below, LEVELS - 1)
-        def _(index):
-            spread[:, pl.ds(pl.multiple_of(index * TILE, TILE), TILE)] = jnp.zeros(
-                (TILE, TILE), BF16
-            )
-            for slot in range(2):
-                term_pieces[slot, index] = jnp.zeros((SEGS, 2, PIECE, HEAD_DIM), BF16)
-
     halves = [pl.ds(part * PIECES_PER_PART, PIECES_PER_PART) for part in range(2)]
+
+    def query_copy(head):
+        span = lanes(head, GROUP)
+        return pltpu.make_async_copy(
+            q_out.at[:, span], grad_queries.at[0, 0, :, span], q_out_sem.at[head]
+        )
+
+    def kv_copy(head):
+        return pltpu.make_async_copy(
+            kv_out.at[:, :, lanes(head)], grad_kv.at[0, 0, :, :, lanes(head)], kv_out_sem.at[head]
+        )
 
     def attend(head, pairs):
         span_all = [pl.ds(group * ROWS, ROWS) for group in range(GROUP)]
@@ -287,9 +290,8 @@
             else:
                 query_sum[...] += moved
         for group, span in enumerate(span_all):
-            grad_queries[0, 0, :, lanes(head * GROUP + group)] = (
-                SCALE * query_sum[:, span].T
-            ).astype(BF16)
+            q_out[:, lanes(head * GROUP + group)] = (SCALE * query_sum[:, span].T).astype(BF16)
+        query_copy(head).start()
 
     def terms_left(head, offset):
         wait_bytes(terms.at[head, offset], b1_send.at[odd(head), offset - 1])
@@ -308,7 +310,7 @@
                 remote(
                     terms.at[head, offset, pl.ds(2 * owner, 2)],
                     term_pieces.at[half(head), offset - 1, me],
-                    b1_send.at[odd(head), offset - 1], b1_recv.at[half(head)],
+                    b1_send.at[odd(head), offset - 1], b1_recv.at[half(head), offset - 1],
                     (level - offset, column),
                 ).start()
 
@@ -317,34 +319,27 @@
 
         @pl.when((level < LEVELS - 1) & (odd(head) == my_parity))
         def _():
-            per_count(
-                below,
-                lambda count: wait_bytes(
-                    term_pieces.at[slot, pl.ds(0, count)], b1_recv.at[slot]
-                ),
-            )
-
-            def add_up(count):
-                received = term_pieces[slot, 0:count]
-                total = jnp.dot(
-                    spread[:, 0:count * TILE],
+            total[...] = jnp.zeros((TILE, 2 * HEAD_DIM), F32)
+
+            @pl.loop(1, below + 1)
+            def _(offset):
+                wait_bytes(term_pieces.at[slot, offset - 1], b1_recv.at[slot, offset - 1])
+                total[...] += jnp.dot(
+                    spread[:, pl.ds(pl.multiple_of((offset - 1) * TILE, TILE), TILE)],
                     jnp.concatenate(
                         [
-                            received[:, :, index].reshape(count * TILE, HEAD_DIM)
+                            term_pieces[slot, offset - 1, :, index].reshape(TILE, HEAD_DIM)
                             for index in range(2)
                         ],
                         axis=1,
                     ),
                     preferred_element_type=F32,
                 )
-                for index in range(2):
-                    final_out[slot, :, index] = total[
-                        :, index * HEAD_DIM:(index + 1) * HEAD_DIM
-                    ].astype(BF16).reshape(SEGS, PIECE, HEAD_DIM)
-
-            pl.when(below <= 2)(lambda: add_up(2))
-            pl.when((below > 2) & (below <= 4))(lambda: add_up(4))
-            pl.when(below > 4)(lambda: add_up(LEVELS - 1))
+
+            for index in range(2):
+                final_out[slot, :, index] = total[
+                    :, index * HEAD_DIM:(index + 1) * HEAD_DIM
+                ].astype(BF16).reshape(SEGS, PIECE, HEAD_DIM)
             landing = final_in.at[head, pl.ds(2 * my_owner, 2)]
             for turn in range(1, SEGS):
                 peer = wrapped(me + turn)
@@ -363,7 +358,8 @@
                     ROWS, HEAD_DIM
                 ).astype(F32)
 
-        grad_kv[0, 0, :, :, lanes(head)] = own[head].astype(BF16)
+        kv_out[:, :, lanes(head)] = own[head].astype(BF16)
+        kv_copy(head).start()
 
     @pl.loop(0, KV_HEADS + 4)
     def _(tick):
@@ -399,6 +395,8 @@
     @pl.loop(0, KV_HEADS)
     def _(head):
         wait_bytes(pieces.at[head, pl.ds(1, SEGS - 1)], p1_send.at[head])
+        query_copy(head).wait()
+        kv_copy(head).wait()
 
     @pl.loop(1, below + 1)
     def _(offset):
@@ -415,7 +413,6 @@
 
 
 def shards(queries, keys_values, grad_out, parents):
-    vmem = pl.BlockSpec(memory_space=pltpu.VMEM)
     smem = pl.BlockSpec(memory_space=pltpu.SMEM)
     hbm = pl.BlockSpec(memory_space=pltpu.HBM)
     dma = pltpu.SemaphoreType.DMA
@@ -442,14 +439,18 @@
         pltpu.VMEM((keys_count, STACK), F32),
         pltpu.VMEM((keys_count, STACK), BF16),
         pltpu.VMEM((keys_count, STACK), BF16),
+        pltpu.VMEM((TILE, 2 * HEAD_DIM), F32),
         pltpu.VMEM((2, SEGS, 2, PIECE, HEAD_DIM), BF16),
         pltpu.VMEM((KV_HEADS,) + tile, BF16),
+        pltpu.VMEM((ROWS, HEADS * HEAD_DIM), BF16),
+        pltpu.VMEM((2, ROWS, KV_HEADS * HEAD_DIM), BF16),
         dma, dma, dma,
         pltpu.SemaphoreType.REGULAR,
         dma((KV_HEADS,)), dma((KV_HEADS,)),
         dma((2, LEVELS - 1)), dma((KV_HEADS,)),
-        dma((2, LEVELS - 1)), dma((2,)),
+        dma((2, LEVELS - 1)), dma((2, LEVELS - 1)),
         dma((2,)), dma((KV_HEADS,)),
+        dma((KV_HEADS,)), dma((KV_HEADS,)),
     ]
     return pl.pallas_call(
         kernel,
@@ -458,7 +459,7 @@
             jax.ShapeDtypeStruct(keys_values.shape, BF16),
         ),
         in_specs=[smem, hbm, hbm, hbm],
-        out_specs=(vmem, vmem),
+        out_specs=(hbm, hbm),
         scratch_shapes=scratch,
         compiler_params=pltpu.CompilerParams(
             collective_id=0, has_side_effects=True, vmem_limit_bytes=56 * 1024 * 1024

time: 68.7 us -> 68.6 us (level)
  no operation moved by 1% of the time
where the time goes in v10:
time: 68.6 us; the launch traced here: 68.4 us
  Pallas kernels  65 us (95%)
  local copies, waits for them, and re-layouts  2.71 us (4%)
    pallas_call x1, Pallas kernels, shards(): pl.pallas_call(kernel, out_shape=(jax.ShapeDtypeStruct(queries.shape, BF1...  65 us
    unnamed x4, local copies, waits for them, and re-layouts  2.71 us

profile of v10, /device:TPU:0, one launch (start us, length us, event | category | flops | bytes accessed | tf_op | source)
XLA Modules:
  0.0 68.4 jit_solution(6272237219535113160)
XLA Ops:
  0.6 65.0 %shard_map.59 = (bf16[1,1,128,2560]{3,2,1,0:T(8,128)(2,1)}, bf16[1,1,2,128,512]{4,3,2,1,0:T(8,128)(2,1)}) custom-call(s32[7,1,16]{2,1,0:T(1,128)} %bitcast.1, bf16[1,1,128,2560]{3,2,1,0:T(8,128)(2,1)} %queries.1, bf16[1,1,2,128,512]{4,3,2,1,0:T(8,128)(2,1)} %keys_values.1, bf16[1,1,128,2560]{3,2,1,0:T(8,128)(2,1)} %grad_out.1), custom_call_target="tpu_custom_call" | custom-call | flops 3355443200 | bytes 8388608 | tf_op jit(solution)/shard_map/pallas_call | solution.py:455
  65.7 0.0 copy-start
  65.7 2.0 %copy.8 = bf16[1,1,128,2560]{3,2,1,0:T(8,128)(2,1)} copy(bf16[1,1,128,2560]{3,2,1,0:T(8,128)(2,1)} %get-tuple-element.4) | data formatting | bytes 1310720
  67.7 0.0 copy-done
  67.7 0.7 %copy.9 = bf16[1,1,2,128,512]{4,3,2,1,0:T(8,128)(2,1)} copy(bf16[1,1,2,128,512]{4,3,2,1,0:T(8,128)(2,1)S(1)} %copy-done) | data formatting | bytes 524288
Async XLA Ops:
  65.7 2.0 %copy-start = (bf16[1,1,2,128,512]{4,3,2,1,0:T(8,128)(2,1)S(1)}, bf16[1,1,2,128,512]{4,3,2,1,0:T(8,128)(2,1)}, u32[]{:S(2)}) copy-start(bf16[1,1,2,128,512]{4,3,2,1,0:T(8,128)(2,1)} %get-tuple-element.5) | copy-start | bytes 786436

commit v11 on v10

--- a/solution.py
+++ b/solution.py
@@ -73,6 +73,7 @@
     my_z, my_x = lax.div(me, 4), lax.rem(me, 4)
     my_parity = odd(my_z + my_x)
     my_owner = 2 * my_z + half(my_x)
+    summed_level = jnp.where(my_parity == 1, LEVELS - 1 - level, level)
 
     def remote(src, dst, send_sem, recv_sem, device):
         return pltpu.make_async_remote_copy(
@@ -110,15 +111,18 @@
     def _(step):
         pl.semaphore_signal(barrier, inc=1, device_id=in_line(step), device_id_type=MESH)
 
-    @pl.loop(0, SEGS)
-    def _(column):
-        anc[0, column] = column
-
-    @pl.loop(1, below + 1)
-    def _(offset):
+    for index, base in enumerate((level, summed_level)):
         @pl.loop(0, SEGS)
         def _(column):
-            anc[offset, column] = anc[offset - 1, parents[level + offset - 1, 0, column]]
+            anc[index, 0, column] = column
+
+        @pl.loop(1, LEVELS - base)
+        def _(offset):
+            @pl.loop(0, SEGS)
+            def _(column):
+                anc[index, offset, column] = anc[
+                    index, offset - 1, parents[base + offset - 1, 0, column]
+                ]
 
     load_kv.wait()
     for head in range(KV_HEADS):
@@ -152,7 +156,7 @@
         ahead = lane - row
         for column in range(SEGS):
             pick[offset - 1, rows_of(column, PIECE), :] = jnp.where(
-                ahead == anc[offset, column] * PIECE, 1.0, 0.0
+                ahead == anc[0, offset, column] * PIECE, 1.0, 0.0
             ).astype(BF16)
 
     def batch_left(head, offset):
@@ -190,7 +194,7 @@
             blocks[head, level + 1] = jnp.zeros((SEGS, PIECE, HEAD_DIM), BF16)
 
     def make_spread():
-        @pl.loop(1, below + 1)
+        @pl.loop(1, LEVELS - summed_level)
         def _(offset):
             lane = lax.broadcasted_iota(jnp.int32, (PIECE, TILE), 1)
             row = lax.broadcasted_iota(jnp.int32, (PIECE, TILE), 0)
@@ -199,7 +203,7 @@
             target = (lane & (PIECE - 1)) - row
             for column in range(SEGS):
                 target = jnp.where(
-                    lane_column == column, target + anc[offset, column] * PIECE, target
+                    lane_column == column, target + anc[1, offset, column] * PIECE, target
                 )
             for column in range(SEGS):
                 spread[rows_of(column, PIECE), span] = jnp.where(
@@ -293,8 +297,18 @@
             q_out[:, lanes(head * GROUP + group)] = (SCALE * query_sum[:, span].T).astype(BF16)
         query_copy(head).start()
 
+    def summing_level(head, offset):
+        target = level - offset
+        return jnp.where(odd(head) == 1, LEVELS - 1 - target, target)
+
+    def stays(head, offset):
+        return (summing_level(head, offset) == level) & (my_parity == odd(head))
+
     def terms_left(head, offset):
-        wait_bytes(terms.at[head, offset], b1_send.at[odd(head), offset - 1])
+        sem = b1_send.at[odd(head), offset - 1]
+        local = stays(head, offset)
+        pl.when(local)(lambda: wait_bytes(terms.at[head, offset, pl.ds(2, SEGS - 2)], sem))
+        pl.when(~local)(lambda: wait_bytes(terms.at[head, offset], sem))
 
     def send_terms(head):
         targets = []
@@ -306,22 +320,29 @@
         @pl.loop(1, level + 1)
         def _(offset):
             pl.when(head > 0)(lambda: terms_left(head - 1, offset))
-            for owner, column in targets:
-                remote(
-                    terms.at[head, offset, pl.ds(2 * owner, 2)],
-                    term_pieces.at[half(head), offset - 1, me],
-                    b1_send.at[odd(head), offset - 1], b1_recv.at[half(head), offset - 1],
-                    (level - offset, column),
-                ).start()
+            host = summing_level(head, offset)
+            local = stays(head, offset)
+            landing = term_pieces.at[half(head), offset - 1, me]
+            arrival = b1_recv.at[half(head), offset - 1]
+            for turn, (owner, column) in enumerate(targets):
+                source = terms.at[head, offset, pl.ds(2 * owner, 2)]
+                copy = remote(
+                    source, landing, b1_send.at[odd(head), offset - 1], arrival, (host, column)
+                )
+                if turn > 0:
+                    copy.start()
+                else:
+                    pl.when(~local)(copy.start)
+                    pl.when(local)(pltpu.make_async_copy(source, landing, arrival).start)
 
     def sum_and_return(head):
         slot = half(head)
 
-        @pl.when((level < LEVELS - 1) & (odd(head) == my_parity))
+        @pl.when((summed_level < LEVELS - 1) & (odd(head) == my_parity))
         def _():
             total[...] = jnp.zeros((TILE, 2 * HEAD_DIM), F32)
 
-            @pl.loop(1, below + 1)
+            @pl.loop(1, LEVELS - summed_level)
             def _(offset):
                 wait_bytes(term_pieces.at[slot, offset - 1], b1_recv.at[slot, offset - 1])
                 total[...] += jnp.dot(
@@ -341,13 +362,21 @@
                     :, index * HEAD_DIM:(index + 1) * HEAD_DIM
                 ].astype(BF16).reshape(SEGS, PIECE, HEAD_DIM)
             landing = final_in.at[head, pl.ds(2 * my_owner, 2)]
+
+            def copy_to(peer):
+                return remote(
+                    final_out.at[slot, peer], landing,
+                    f_send.at[slot], f_recv.at[head], (summed_level, peer),
+                )
+
             for turn in range(1, SEGS):
-                peer = wrapped(me + turn)
-                remote(
-                    final_out.at[slot, peer], landing,
-                    f_send.at[slot], f_recv.at[head], (level, peer),
+                copy_to(wrapped(me + turn)).start()
+            pl.when(my_parity == 1)(lambda: copy_to(me).start())
+            pl.when(my_parity == 0)(
+                lambda: pltpu.make_async_copy(
+                    final_out.at[slot, me], landing, f_recv.at[head]
                 ).start()
-            pltpu.make_async_copy(final_out.at[slot, me], landing, f_recv.at[head]).start()
+            )
 
     def store(head):
         @pl.when(level < LEVELS - 1)
@@ -372,14 +401,6 @@
             make_spread()
             load_q.wait()
             load_g.wait()
-
-        @pl.when((tick >= 3) & (tick < KV_HEADS + 3))
-        def _():
-            sum_and_return(tick - 3)
-
-        @pl.when(tick >= 4)
-        def _():
-            store(tick - 4)
 
         @pl.when((tick >= 1) & (tick < KV_HEADS + 1))
         def _():
@@ -392,6 +413,14 @@
                 pl.when(half(level) == pairs - 1)(functools.partial(attend, head, pairs))
             send_terms(head)
 
+        @pl.when((tick >= 3) & (tick < KV_HEADS + 3))
+        def _():
+            sum_and_return(tick - 3)
+
+        @pl.when(tick >= 4)
+        def _():
+            store(tick - 4)
+
     @pl.loop(0, KV_HEADS)
     def _(head):
         wait_bytes(pieces.at[head, pl.ds(1, SEGS - 1)], p1_send.at[head])
@@ -406,10 +435,13 @@
     def _(offset):
         terms_left(KV_HEADS - 1, offset)
 
-    @pl.when(level < LEVELS - 1)
+    @pl.when(summed_level < LEVELS - 1)
     def _():
         for slot in range(2):
             wait_bytes(final_out.at[slot, pl.ds(1, SEGS - 1)], f_send.at[slot])
+            pl.when(my_parity == 1)(
+                functools.partial(wait_bytes, final_out.at[slot, 0], f_send.at[slot])
+            )
 
 
 def shards(queries, keys_values, grad_out, parents):
@@ -419,7 +451,7 @@
     tile = (SEGS, PIECE, HEAD_DIM)
     keys_count = LEVELS * ROWS
     scratch = [
-        pltpu.SMEM((LEVELS, SEGS), jnp.int32),
+        pltpu.SMEM((2, LEVELS, SEGS), jnp.int32),
         pltpu.VMEM((LEVELS - 1, TILE, TILE), BF16),
         pltpu.VMEM((TILE, (LEVELS - 1) * TILE), BF16),
         pltpu.VMEM(keys_values.shape, BF16),

time: 68.6 us -> 76.8 us (1.12); the launches traced: 68.4 us -> 75.6 us
  Pallas kernels: 65 us -> 72.2 us
    pallas_call x1, Pallas kernels: 65 us -> 72.2 us  [shards(): pl.pallas_call(kernel, out_shape=(jax.ShapeDtypeStruct(queries.shape, BF1...]
where the time goes in v11:
time: 76.8 us; the launch traced here: 75.6 us
  Pallas kernels  72.2 us (94%)
  local copies, waits for them, and re-layouts  2.71 us (4%)
    pallas_call x1, Pallas kernels, shards(): pl.pallas_call(kernel, out_shape=(jax.ShapeDtypeStruct(queries.shape, BF1...  72.2 us
    unnamed x4, local copies, waits for them, and re-layouts  2.71 us

profile of v11, /device:TPU:0, one launch (start us, length us, event | category | flops | bytes accessed | tf_op | source)
XLA Modules:
  0.0 75.6 jit_solution(8900702694858197692)
XLA Ops:
  0.6 72.2 %shard_map.59 = (bf16[1,1,128,2560]{3,2,1,0:T(8,128)(2,1)}, bf16[1,1,2,128,512]{4,3,2,1,0:T(8,128)(2,1)}) custom-call(s32[7,1,16]{2,1,0:T(1,128)} %bitcast.1, bf16[1,1,128,2560]{3,2,1,0:T(8,128)(2,1)} %queries.1, bf16[1,1,2,128,512]{4,3,2,1,0:T(8,128)(2,1)} %keys_values.1, bf16[1,1,128,2560]{3,2,1,0:T(8,128)(2,1)} %grad_out.1), custom_call_target="tpu_custom_call" | custom-call | flops 3355443200 | bytes 8388608 | tf_op jit(solution)/shard_map/pallas_call | solution.py:487
  72.9 0.0 copy-start
  72.9 2.0 %copy.8 = bf16[1,1,128,2560]{3,2,1,0:T(8,128)(2,1)} copy(bf16[1,1,128,2560]{3,2,1,0:T(8,128)(2,1)} %get-tuple-element.4) | data formatting | bytes 1310720
  74.9 0.0 copy-done
  74.9 0.7 copy.9
Async XLA Ops:
  72.9 2.0 %copy-start = (bf16[1,1,2,128,512]{4,3,2,1,0:T(8,128)(2,1)S(1)}, bf16[1,1,2,128,512]{4,3,2,1,0:T(8,128)(2,1)}, u32[]{:S(2)}) copy-start(bf16[1,1,2,128,512]{4,3,2,1,0:T(8,128)(2,1)} %get-tuple-element.5) | copy-start | bytes 786436

commit v12 on v10

--- a/solution.py
+++ b/solution.py
@@ -63,9 +63,9 @@
     parents, queries, keys_values, grad_out, grad_queries, grad_kv,
     anc, pick, spread, kv_in, q_in, g_in, kv_stage, pieces, chosen, blocks,
     terms, term_pieces, own, stacks, turned, query_sum, logits, grad_probs,
-    probs, grad_logits, total, final_out, final_in, q_out, kv_out,
+    probs, grad_logits, total, final_out, final_in,
     kv_sem, q_sem, g_sem, ready, p1_send, p1_recv, p3_send, p3_recv, b1_send, b1_recv,
-    f_send, f_recv, q_out_sem, kv_out_sem,
+    f_send, f_recv,
 ):
     level = lax.axis_index("depth")
     me = lax.axis_index("seg")
@@ -207,17 +207,6 @@
                 ).astype(BF16)
 
     halves = [pl.ds(part * PIECES_PER_PART, PIECES_PER_PART) for part in range(2)]
-
-    def query_copy(head):
-        span = lanes(head, GROUP)
-        return pltpu.make_async_copy(
-            q_out.at[:, span], grad_queries.at[0, 0, :, span], q_out_sem.at[head]
-        )
-
-    def kv_copy(head):
-        return pltpu.make_async_copy(
-            kv_out.at[:, :, lanes(head)], grad_kv.at[0, 0, :, :, lanes(head)], kv_out_sem.at[head]
-        )
 
     def attend(head, pairs):
         span_all = [pl.ds(group * ROWS, ROWS) for group in range(GROUP)]
@@ -290,8 +279,9 @@
             else:
                 query_sum[...] += moved
         for group, span in enumerate(span_all):
-            q_out[:, lanes(head * GROUP + group)] = (SCALE * query_sum[:, span].T).astype(BF16)
-        query_copy(head).start()
+            grad_queries[0, 0, :, lanes(head * GROUP + group)] = (
+                SCALE * query_sum[:, span].T
+            ).astype(BF16)
 
     def terms_left(head, offset):
         wait_bytes(terms.at[head, offset], b1_send.at[odd(head), offset - 1])
@@ -358,8 +348,7 @@
                     ROWS, HEAD_DIM
                 ).astype(F32)
 
-        kv_out[:, :, lanes(head)] = own[head].astype(BF16)
-        kv_copy(head).start()
+        grad_kv[0, 0, :, :, lanes(head)] = own[head].astype(BF16)
 
     @pl.loop(0, KV_HEADS + 4)
     def _(tick):
@@ -395,8 +384,6 @@
     @pl.loop(0, KV_HEADS)
     def _(head):
         wait_bytes(pieces.at[head, pl.ds(1, SEGS - 1)], p1_send.at[head])
-        query_copy(head).wait()
-        kv_copy(head).wait()
 
     @pl.loop(1, below + 1)
     def _(offset):
@@ -414,6 +401,7 @@
 
 def shards(queries, keys_values, grad_out, parents):
     smem = pl.BlockSpec(memory_space=pltpu.SMEM)
+    vmem = pl.BlockSpec(memory_space=pltpu.VMEM)
     hbm = pl.BlockSpec(memory_space=pltpu.HBM)
     dma = pltpu.SemaphoreType.DMA
     tile = (SEGS, PIECE, HEAD_DIM)
@@ -442,15 +430,12 @@
         pltpu.VMEM((TILE, 2 * HEAD_DIM), F32),
         pltpu.VMEM((2, SEGS, 2, PIECE, HEAD_DIM), BF16),
         pltpu.VMEM((KV_HEADS,) + tile, BF16),
-        pltpu.VMEM((ROWS, HEADS * HEAD_DIM), BF16),
-        pltpu.VMEM((2, ROWS, KV_HEADS * HEAD_DIM), BF16),
         dma, dma, dma,
         pltpu.SemaphoreType.REGULAR,
         dma((KV_HEADS,)), dma((KV_HEADS,)),
         dma((2, LEVELS - 1)), dma((KV_HEADS,)),
         dma((2, LEVELS - 1)), dma((2, LEVELS - 1)),
         dma((2,)), dma((KV_HEADS,)),
-        dma((KV_HEADS,)), dma((KV_HEADS,)),
     ]
     return pl.pallas_call(
         kernel,
@@ -459,10 +444,10 @@
             jax.ShapeDtypeStruct(keys_values.shape, BF16),
         ),
         in_specs=[smem, hbm, hbm, hbm],
-        out_specs=(hbm, hbm),
+        out_specs=(vmem, vmem),
         scratch_shapes=scratch,
         compiler_params=pltpu.CompilerParams(
-            collective_id=0, has_side_effects=True, vmem_limit_bytes=56 * 1024 * 1024
+            collective_id=0, has_side_effects=True, vmem_limit_bytes=105 * 512 * 1024
         ),
         cost_estimate=pl.CostEstimate(
             flops=5 * 2 * HEADS * LEVELS * ROWS * ROWS * HEAD_DIM,

time: 68.6 us -> 68.1 us (level)
  Pallas kernels: 65 us -> 64.1 us
    pallas_call x1, Pallas kernels: 65 us -> 64.1 us  [shards(): pl.pallas_call(kernel, out_shape=(jax.ShapeDtypeStruct(queries.shape, BF1...]
    unnamed x4 -> x6, local copies, waits for them, and re-layouts: 2.71 us -> 3.17 us
where the time goes in v12:
time: 68.1 us; the launch traced here: 67.9 us
  Pallas kernels  64.1 us (94%)
  local copies, waits for them, and re-layouts  3.17 us (5%)
    pallas_call x1, Pallas kernels, shards(): pl.pallas_call(kernel, out_shape=(jax.ShapeDtypeStruct(queries.shape, BF1...  64.1 us
    unnamed x6, local copies, waits for them, and re-layouts  3.17 us

profile of v12, /device:TPU:0, one launch (start us, length us, event | category | flops | bytes accessed | tf_op | source)
XLA Modules:
  0.0 67.9 jit_solution(9866619130096865834)
XLA Ops:
  0.6 0.0 copy-start
  0.6 0.9 %copy-done = bf16[1,1,2,128,512]{4,3,2,1,0:T(8,128)(2,1)S(1)} copy-done((bf16[1,1,2,128,512]{4,3,2,1,0:T(8,128)(2,1)S(1)}, bf16[1,1,2,128,512]{4,3,2,1,0:T(8,128)(2,1)}, u32[]{:S(2)}) %copy-start) | copy-done | bytes 262168
  1.6 0.0 copy-start.1
  1.6 0.7 %copy-done.1 = s32[7,16,1]{1,2,0:T(1,128)S(1)} copy-done((s32[7,16,1]{1,2,0:T(1,128)S(1)}, s32[7,16,1]{1,2,0:T(1,128)}, u32[]{:S(2)}) %copy-start.1) | copy-done | bytes 472
  2.3 64.1 %shard_map.59 = (bf16[1,1,128,2560]{3,2,1,0:T(8,128)(2,1)S(1)}, bf16[1,1,2,128,512]{4,3,2,1,0:T(8,128)(2,1)S(1)}) custom-call(s32[7,1,16]{2,1,0:T(1,128)S(1)} %bitcast.1, bf16[1,1,128,2560]{3,2,1,0:T(8,128)(2,1)} %queries.1, bf16[1,1,2,128,512]{4,3,2,1,0:T(8,128)(2,1)S(1)} %copy-done, bf16[1,1,128,2560]{3,2,1,0:T(8,128)(2,1)} %grad_out.1), custom_call_target="tpu_custom_call" | custom-call | flops 3355443200 | bytes 8388608 | tf_op jit(solution)/shard_map/pallas_call | solution.py:440
  66.4 0.8 %copy.8 = bf16[1,1,128,2560]{3,2,1,0:T(8,128)(2,1)} copy(bf16[1,1,128,2560]{3,2,1,0:T(8,128)(2,1)S(1)} %get-tuple-element.4) | data formatting | bytes 1310720
  67.2 0.7 %copy.9 = bf16[1,1,2,128,512]{4,3,2,1,0:T(8,128)(2,1)} copy(bf16[1,1,2,128,512]{4,3,2,1,0:T(8,128)(2,1)S(1)} %get-tuple-element.5) | data formatting | bytes 524288
Async XLA Ops:
  0.6 1.0 %copy-start = (bf16[1,1,2,128,512]{4,3,2,1,0:T(8,128)(2,1)S(1)}, bf16[1,1,2,128,512]{4,3,2,1,0:T(8,128)(2,1)}, u32[]{:S(2)}) copy-start(bf16[1,1,2,128,512]{4,3,2,1,0:T(8,128)(2,1)} %keys_values.1) | copy-start | bytes 786436
  1.6 0.7 %copy-start.1 = (s32[7,16,1]{1,2,0:T(1,128)S(1)}, s32[7,16,1]{1,2,0:T(1,128)}, u32[]{:S(2)}) copy-start(s32[7,16,1]{1,2,0:T(1,128)} %param.7) | copy-start | bytes 1348

commit v13 on v12

--- a/solution.py
+++ b/solution.py
@@ -158,18 +158,39 @@
     def batch_left(head, offset):
         wait_bytes(chosen.at[head, offset - 1], p3_send.at[odd(head), offset - 1])
 
-    def pick_and_send(head):
+    def pick_up(head):
         wait_bytes(pieces.at[head], p1_recv.at[head])
         pl.when(head < KV_HEADS - 1)(lambda: spread_out(head + 1))
+
+        def products(count):
+            found = jnp.dot(
+                pick[0:count].reshape(count * TILE, TILE),
+                pieces[head].reshape(TILE, HEAD_DIM), preferred_element_type=F32,
+            )
+            chosen[head, 0:count] = found.astype(BF16).reshape(count, SEGS, PIECE, HEAD_DIM)
+
+        pl.when((below > 0) & (below <= 2))(lambda: products(2))
+        pl.when((below > 2) & (below <= 4))(lambda: products(4))
+        pl.when(below > 4)(lambda: products(LEVELS - 1))
+
+    def send_pieces(head):
+        @pl.when(head == 0)
+        def _():
+            wait_bytes(pieces.at[0], p1_recv.at[0])
+            spread_out(1)
 
         @pl.loop(1, below + 1)
         def _(step):
             offset = jnp.where(head == 0, below + 1 - step, step)
-            found = jnp.dot(
-                pick[offset - 1], pieces[head].reshape(TILE, HEAD_DIM),
-                preferred_element_type=F32,
-            )
-            chosen[head, offset - 1] = found.astype(BF16).reshape(SEGS, PIECE, HEAD_DIM)
+
+            @pl.when(head == 0)
+            def _():
+                found = jnp.dot(
+                    pick[offset - 1], pieces[0].reshape(TILE, HEAD_DIM),
+                    preferred_element_type=F32,
+                )
+                chosen[0, offset - 1] = found.astype(BF16).reshape(SEGS, PIECE, HEAD_DIM)
+
             pl.when(head > 0)(lambda: batch_left(head - 1, offset))
             for turn in range(SEGS):
                 column = wrapped(me + turn)
@@ -354,7 +375,7 @@
     def _(tick):
         @pl.when(tick < KV_HEADS)
         def _():
-            pick_and_send(tick)
+            send_pieces(tick)
 
         @pl.when(tick == 0)
         def _():
@@ -380,6 +401,10 @@
             for pairs in range(1, LEVELS // 2 + 1):
                 pl.when(half(level) == pairs - 1)(functools.partial(attend, head, pairs))
             send_terms(head)
+
+        @pl.when(tick < KV_HEADS - 1)
+        def _():
+            pick_up(tick + 1)
 
     @pl.loop(0, KV_HEADS)
     def _(head):

time: 68.1 us -> 68.6 us (level)
  no operation moved by 1% of the time
where the time goes in v13:
time: 68.6 us; the launch traced here: 68.4 us
  Pallas kernels  64.6 us (94%)
  local copies, waits for them, and re-layouts  3.17 us (5%)
    pallas_call x1, Pallas kernels, shards(): pl.pallas_call(kernel, out_shape=(jax.ShapeDtypeStruct(queries.shape, BF1...  64.6 us
    unnamed x6, local copies, waits for them, and re-layouts  3.17 us

profile of v13, /device:TPU:0, one launch (start us, length us, event | category | flops | bytes accessed | tf_op | source)
XLA Modules:
  0.0 68.4 jit_solution(3455255229694843078)
XLA Ops:
  0.6 0.0 copy-start
  0.6 0.9 %copy-done = bf16[1,1,2,128,512]{4,3,2,1,0:T(8,128)(2,1)S(1)} copy-done((bf16[1,1,2,128,512]{4,3,2,1,0:T(8,128)(2,1)S(1)}, bf16[1,1,2,128,512]{4,3,2,1,0:T(8,128)(2,1)}, u32[]{:S(2)}) %copy-start) | copy-done | bytes 262168
  1.6 0.0 copy-start.1
  1.6 0.7 copy-done.1
  2.3 64.6 %shard_map.59 = (bf16[1,1,128,2560]{3,2,1,0:T(8,128)(2,1)S(1)}, bf16[1,1,2,128,512]{4,3,2,1,0:T(8,128)(2,1)S(1)}) custom-call(s32[7,1,16]{2,1,0:T(1,128)S(1)} %bitcast.1, bf16[1,1,128,2560]{3,2,1,0:T(8,128)(2,1)} %queries.1, bf16[1,1,2,128,512]{4,3,2,1,0:T(8,128)(2,1)S(1)} %copy-done, bf16[1,1,128,2560]{3,2,1,0:T(8,128)(2,1)} %grad_out.1), custom_call_target="tpu_custom_call" | custom-call | flops 3355443200 | bytes 8388608 | tf_op jit(solution)/shard_map/pallas_call | solution.py:465
  66.9 0.8 %copy.8 = bf16[1,1,128,2560]{3,2,1,0:T(8,128)(2,1)} copy(bf16[1,1,128,2560]{3,2,1,0:T(8,128)(2,1)S(1)} %get-tuple-element.4) | data formatting | bytes 1310720
  67.7 0.7 %copy.9 = bf16[1,1,2,128,512]{4,3,2,1,0:T(8,128)(2,1)} copy(bf16[1,1,2,128,512]{4,3,2,1,0:T(8,128)(2,1)S(1)} %get-tuple-element.5) | data formatting | bytes 524288
Async XLA Ops:
  0.6 1.0 %copy-start = (bf16[1,1,2,128,512]{4,3,2,1,0:T(8,128)(2,1)S(1)}, bf16[1,1,2,128,512]{4,3,2,1,0:T(8,128)(2,1)}, u32[]{:S(2)}) copy-start(bf16[1,1,2,128,512]{4,3,2,1,0:T(8,128)(2,1)} %keys_values.1) | copy-start | bytes 786436
  1.6 0.7 %copy-start.1 = (s32[7,16,1]{1,2,0:T(1,128)S(1)}, s32[7,16,1]{1,2,0:T(1,128)}, u32[]{:S(2)}) copy-start(s32[7,16,1]{1,2,0:T(1,128)} %param.7) | copy-start | bytes 1348

commit v14 on v12

--- a/solution.py
+++ b/solution.py
@@ -170,7 +170,7 @@
                 preferred_element_type=F32,
             )
             chosen[head, offset - 1] = found.astype(BF16).reshape(SEGS, PIECE, HEAD_DIM)
-            pl.when(head > 0)(lambda: batch_left(head - 1, offset))
+            pl.when(head > 1)(lambda: batch_left(head - 2, offset))
             for turn in range(SEGS):
                 column = wrapped(me + turn)
                 remote(
@@ -387,6 +387,7 @@
 
     @pl.loop(1, below + 1)
     def _(offset):
+        batch_left(KV_HEADS - 2, offset)
         batch_left(KV_HEADS - 1, offset)
 
     @pl.loop(1, level + 1)

time: 68.1 us -> 69 us (1.013)
  Pallas kernels: 64.1 us -> 65.1 us
    pallas_call x1, Pallas kernels: 64.1 us -> 65.1 us  [shards(): pl.pallas_call(kernel, out_shape=(jax.ShapeDtypeStruct(queries.shape, BF1...]
where the time goes in v14:
time: 69 us; the launch traced here: 68.9 us
  Pallas kernels  65.1 us (94%)
  local copies, waits for them, and re-layouts  3.17 us (5%)
    pallas_call x1, Pallas kernels, shards(): pl.pallas_call(kernel, out_shape=(jax.ShapeDtypeStruct(queries.shape, BF1...  65.1 us
    unnamed x6, local copies, waits for them, and re-layouts  3.17 us

profile of v14, /device:TPU:0, one launch (start us, length us, event | category | flops | bytes accessed | tf_op | source)
XLA Modules:
  0.0 68.9 jit_solution(4974371168272547276)
XLA Ops:
  0.6 0.0 copy-start
  0.6 0.9 %copy-done = bf16[1,1,2,128,512]{4,3,2,1,0:T(8,128)(2,1)S(1)} copy-done((bf16[1,1,2,128,512]{4,3,2,1,0:T(8,128)(2,1)S(1)}, bf16[1,1,2,128,512]{4,3,2,1,0:T(8,128)(2,1)}, u32[]{:S(2)}) %copy-start) | copy-done | bytes 262168
  1.6 0.0 copy-start.1
  1.6 0.7 copy-done.1
  2.3 65.1 %shard_map.59 = (bf16[1,1,128,2560]{3,2,1,0:T(8,128)(2,1)S(1)}, bf16[1,1,2,128,512]{4,3,2,1,0:T(8,128)(2,1)S(1)}) custom-call(s32[7,1,16]{2,1,0:T(1,128)S(1)} %bitcast.1, bf16[1,1,128,2560]{3,2,1,0:T(8,128)(2,1)} %queries.1, bf16[1,1,2,128,512]{4,3,2,1,0:T(8,128)(2,1)S(1)} %copy-done, bf16[1,1,128,2560]{3,2,1,0:T(8,128)(2,1)} %grad_out.1), custom_call_target="tpu_custom_call" | custom-call | flops 3355443200 | bytes 8388608 | tf_op jit(solution)/shard_map/pallas_call | solution.py:441
  67.3 0.8 %copy.8 = bf16[1,1,128,2560]{3,2,1,0:T(8,128)(2,1)} copy(bf16[1,1,128,2560]{3,2,1,0:T(8,128)(2,1)S(1)} %get-tuple-element.4) | data formatting | bytes 1310720
  68.2 0.7 %copy.9 = bf16[1,1,2,128,512]{4,3,2,1,0:T(8,128)(2,1)} copy(bf16[1,1,2,128,512]{4,3,2,1,0:T(8,128)(2,1)S(1)} %get-tuple-element.5) | data formatting | bytes 524288
Async XLA Ops:
  0.6 1.0 %copy-start = (bf16[1,1,2,128,512]{4,3,2,1,0:T(8,128)(2,1)S(1)}, bf16[1,1,2,128,512]{4,3,2,1,0:T(8,128)(2,1)}, u32[]{:S(2)}) copy-start(bf16[1,1,2,128,512]{4,3,2,1,0:T(8,128)(2,1)} %keys_values.1) | copy-start | bytes 786436
  1.6 0.7 copy-start.1

commit v15 on v12

--- a/solution.py
+++ b/solution.py
@@ -48,11 +48,6 @@
 
 def rows_of(index, count):
     return pl.ds(pl.multiple_of(index * count, count), count)
-
-
-def owner_column(owner, parity):
-    z = half(owner)
-    return 4 * z + 2 * odd(owner) + odd(z + parity)
 
 
 def fold(tile):
@@ -74,6 +69,12 @@
     my_parity = odd(my_z + my_x)
     my_owner = 2 * my_z + half(my_x)
 
+    def around(index):
+        return jnp.where(index >= 4, index - 4, index)
+
+    def shifted(dz, dx):
+        return 4 * around(my_z + dz) + around(my_x + dx)
+
     def remote(src, dst, send_sem, recv_sem, device):
         return pltpu.make_async_remote_copy(
             src_ref=src, dst_ref=dst, send_sem=send_sem, recv_sem=recv_sem,
@@ -130,7 +131,7 @@
 
     def spread_out(head):
         for turn in range(1, SEGS):
-            peer = wrapped(me + turn)
+            peer = shifted(turn // 4, turn % 4)
             remote(
                 kv_stage.at[head, peer], pieces.at[head, me],
                 p1_send.at[head], p1_recv.at[head], (level, peer),
@@ -172,7 +173,7 @@
             chosen[head, offset - 1] = found.astype(BF16).reshape(SEGS, PIECE, HEAD_DIM)
             pl.when(head > 0)(lambda: batch_left(head - 1, offset))
             for turn in range(SEGS):
-                column = wrapped(me + turn)
+                column = shifted(turn // 4, turn % 4)
                 remote(
                     chosen.at[head, offset - 1, column], blocks.at[head, offset, me],
                     p3_send.at[odd(head), offset - 1], p3_recv.at[head],
@@ -288,10 +289,11 @@
 
     def send_terms(head):
         targets = []
+        skew = jnp.where(my_parity == odd(head), 0, 1)
         for turn in range(OWNERS):
-            owner = my_owner + turn
-            owner = jnp.where(owner >= OWNERS, owner - OWNERS, owner)
-            targets.append((owner, owner_column(owner, odd(head))))
+            z = around(my_z + turn // 2)
+            x = around(my_x + (0, 2, 1, 3)[turn % 4] + skew)
+            targets.append((2 * z + half(x), 4 * z + x))
 
         @pl.loop(1, level + 1)
         def _(offset):
@@ -332,7 +334,7 @@
                 ].astype(BF16).reshape(SEGS, PIECE, HEAD_DIM)
             landing = final_in.at[head, pl.ds(2 * my_owner, 2)]
             for turn in range(1, SEGS):
-                peer = wrapped(me + turn)
+                peer = shifted(turn // 4, turn % 4)
                 remote(
                     final_out.at[slot, peer], landing,
                     f_send.at[slot], f_recv.at[head], (level, peer),

time: 68.1 us -> 68 us (level)
  no operation moved by 1% of the time
where the time goes in v15:
time: 68 us; the launch traced here: 67.8 us
  Pallas kernels  64 us (94%)
  local copies, waits for them, and re-layouts  3.17 us (5%)
    pallas_call x1, Pallas kernels, shards(): pl.pallas_call(kernel, out_shape=(jax.ShapeDtypeStruct(queries.shape, BF1...  64 us
    unnamed x6, local copies, waits for them, and re-layouts  3.17 us

profile of v15, /device:TPU:0, one launch (start us, length us, event | category | flops | bytes accessed | tf_op | source)
XLA Modules:
  0.0 67.8 jit_solution(15473086714637929745)
XLA Ops:
  0.6 0.0 copy-start
  0.6 0.9 %copy-done = bf16[1,1,2,128,512]{4,3,2,1,0:T(8,128)(2,1)S(1)} copy-done((bf16[1,1,2,128,512]{4,3,2,1,0:T(8,128)(2,1)S(1)}, bf16[1,1,2,128,512]{4,3,2,1,0:T(8,128)(2,1)}, u32[]{:S(2)}) %copy-start) | copy-done | bytes 262168
  1.6 0.0 copy-start.1
  1.6 0.7 %copy-done.1 = s32[7,16,1]{1,2,0:T(1,128)S(1)} copy-done((s32[7,16,1]{1,2,0:T(1,128)S(1)}, s32[7,16,1]{1,2,0:T(1,128)}, u32[]{:S(2)}) %copy-start.1) | copy-done | bytes 472
  2.3 64.0 %shard_map.59 = (bf16[1,1,128,2560]{3,2,1,0:T(8,128)(2,1)S(1)}, bf16[1,1,2,128,512]{4,3,2,1,0:T(8,128)(2,1)S(1)}) custom-call(s32[7,1,16]{2,1,0:T(1,128)S(1)} %bitcast.1, bf16[1,1,128,2560]{3,2,1,0:T(8,128)(2,1)} %queries.1, bf16[1,1,2,128,512]{4,3,2,1,0:T(8,128)(2,1)S(1)} %copy-done, bf16[1,1,128,2560]{3,2,1,0:T(8,128)(2,1)} %grad_out.1), custom_call_target="tpu_custom_call" | custom-call | flops 3355443200 | bytes 8388608 | tf_op jit(solution)/shard_map/pallas_call | solution.py:442
  66.2 0.8 %copy.8 = bf16[1,1,128,2560]{3,2,1,0:T(8,128)(2,1)} copy(bf16[1,1,128,2560]{3,2,1,0:T(8,128)(2,1)S(1)} %get-tuple-element.4) | data formatting | bytes 1310720
  67.1 0.7 %copy.9 = bf16[1,1,2,128,512]{4,3,2,1,0:T(8,128)(2,1)} copy(bf16[1,1,2,128,512]{4,3,2,1,0:T(8,128)(2,1)S(1)} %get-tuple-element.5) | data formatting | bytes 524288
Async XLA Ops:
  0.6 1.0 %copy-start = (bf16[1,1,2,128,512]{4,3,2,1,0:T(8,128)(2,1)S(1)}, bf16[1,1,2,128,512]{4,3,2,1,0:T(8,128)(2,1)}, u32[]{:S(2)}) copy-start(bf16[1,1,2,128,512]{4,3,2,1,0:T(8,128)(2,1)} %keys_values.1) | copy-start | bytes 786436
  1.6 0.7 %copy-start.1 = (s32[7,16,1]{1,2,0:T(1,128)S(1)}, s32[7,16,1]{1,2,0:T(1,128)}, u32[]{:S(2)}) copy-start(s32[7,16,1]{1,2,0:T(1,128)} %param.7) | copy-start | bytes 1348

commit v16 on v15

--- a/solution.py
+++ b/solution.py
@@ -364,14 +364,6 @@
             load_q.wait()
             load_g.wait()
 
-        @pl.when((tick >= 3) & (tick < KV_HEADS + 3))
-        def _():
-            sum_and_return(tick - 3)
-
-        @pl.when(tick >= 4)
-        def _():
-            store(tick - 4)
-
         @pl.when((tick >= 1) & (tick < KV_HEADS + 1))
         def _():
             head = tick - 1
@@ -382,6 +374,14 @@
             for pairs in range(1, LEVELS // 2 + 1):
                 pl.when(half(level) == pairs - 1)(functools.partial(attend, head, pairs))
             send_terms(head)
+
+        @pl.when((tick >= 3) & (tick < KV_HEADS + 3))
+        def _():
+            sum_and_return(tick - 3)
+
+        @pl.when(tick >= 4)
+        def _():
+            store(tick - 4)
 
     @pl.loop(0, KV_HEADS)
     def _(head):

time: 68 us -> 67.8 us (level)
  no operation moved by 1% of the time
where the time goes in v16:
time: 67.8 us; the launch traced here: 67.6 us
  Pallas kernels  63.8 us (94%)
  local copies, waits for them, and re-layouts  3.17 us (5%)
    pallas_call x1, Pallas kernels, shards(): pl.pallas_call(kernel, out_shape=(jax.ShapeDtypeStruct(queries.shape, BF1...  63.8 us
    unnamed x6, local copies, waits for them, and re-layouts  3.17 us

profile of v16, /device:TPU:0, one launch (start us, length us, event | category | flops | bytes accessed | tf_op | source)
XLA Modules:
  0.0 67.6 jit_solution(14774506514481779871)
XLA Ops:
  0.6 0.0 copy-start
  0.6 0.9 %copy-done = bf16[1,1,2,128,512]{4,3,2,1,0:T(8,128)(2,1)S(1)} copy-done((bf16[1,1,2,128,512]{4,3,2,1,0:T(8,128)(2,1)S(1)}, bf16[1,1,2,128,512]{4,3,2,1,0:T(8,128)(2,1)}, u32[]{:S(2)}) %copy-start) | copy-done | bytes 262168
  1.6 0.0 copy-start.1
  1.6 0.7 %copy-done.1 = s32[7,16,1]{1,2,0:T(1,128)S(1)} copy-done((s32[7,16,1]{1,2,0:T(1,128)S(1)}, s32[7,16,1]{1,2,0:T(1,128)}, u32[]{:S(2)}) %copy-start.1) | copy-done | bytes 472
  2.3 63.8 %shard_map.59 = (bf16[1,1,128,2560]{3,2,1,0:T(8,128)(2,1)S(1)}, bf16[1,1,2,128,512]{4,3,2,1,0:T(8,128)(2,1)S(1)}) custom-call(s32[7,1,16]{2,1,0:T(1,128)S(1)} %bitcast.1, bf16[1,1,128,2560]{3,2,1,0:T(8,128)(2,1)} %queries.1, bf16[1,1,2,128,512]{4,3,2,1,0:T(8,128)(2,1)S(1)} %copy-done, bf16[1,1,128,2560]{3,2,1,0:T(8,128)(2,1)} %grad_out.1), custom_call_target="tpu_custom_call" | custom-call | flops 3355443200 | bytes 8388608 | tf_op jit(solution)/shard_map/pallas_call | solution.py:442
  66.1 0.8 %copy.8 = bf16[1,1,128,2560]{3,2,1,0:T(8,128)(2,1)} copy(bf16[1,1,128,2560]{3,2,1,0:T(8,128)(2,1)S(1)} %get-tuple-element.4) | data formatting | bytes 1310720
  66.9 0.7 %copy.9 = bf16[1,1,2,128,512]{4,3,2,1,0:T(8,128)(2,1)} copy(bf16[1,1,2,128,512]{4,3,2,1,0:T(8,128)(2,1)S(1)} %get-tuple-element.5) | data formatting | bytes 524288
Async XLA Ops:
  0.6 1.0 %copy-start = (bf16[1,1,2,128,512]{4,3,2,1,0:T(8,128)(2,1)S(1)}, bf16[1,1,2,128,512]{4,3,2,1,0:T(8,128)(2,1)}, u32[]{:S(2)}) copy-start(bf16[1,1,2,128,512]{4,3,2,1,0:T(8,128)(2,1)} %keys_values.1) | copy-start | bytes 786436
  1.6 0.7 %copy-start.1 = (s32[7,16,1]{1,2,0:T(1,128)S(1)}, s32[7,16,1]{1,2,0:T(1,128)}, u32[]{:S(2)}) copy-start(s32[7,16,1]{1,2,0:T(1,128)} %param.7) | copy-start | bytes 1348
